TPU v7x, 32 devices: a whole 2x2x4 slice. The times are simulated.
32 devices in a mesh: groups: 2 (over y), tensor: 4 (over z), store: 4 (over x, core).
Axes of the slice: x: 2, y: 2, z: 4, core: 2. Of those that a mesh axis runs over, the one named last changes fastest.
Arguments:
- hidden_activations: bfloat16 [2048, 28672], P('groups', 'tensor'), parts along dimension 0, may hold values from -6 to 6
- down_matrix: bfloat16 [28672, 8192], P('tensor', 'store'), may hold values from -0.03125 to 0.03125
- adapter_input_factor: bfloat16 [32, 28672, 128], P(('groups', 'store'), 'tensor'), parts along dimension 0, may hold values from -0.03125 to 0.03125
- adapter_output_factor: bfloat16 [32, 128, 8192], P(('groups', 'store'), 'tensor'), parts along dimension 0, may hold values from -0.5 to 0.5
- token_requests: int32 [2048], P('groups'), parts along dimension 0, may hold values from 0 to 3, never falling along the last dimension, each value on 1 to 512 neighbouring positions
- request_adapters: int32 [8], P('groups'), parts along dimension 0, may hold values from 0 to 15
- adapter_ranks: int32 [32], P('groups'), parts along dimension 0, may hold values from 16 to 128, as said below
- adapter_store_slot: int32 [32], P('groups'), parts along dimension 0, may hold values from 0 to 15, each once
Outputs:
- mixed: bfloat16 [2048, 8192], P(('groups', 'tensor'), 'store'), parts along dimension 0
There are 2 independent parts, one for each index of `groups`. A program takes and returns all parts, laid end to end along the dimension named above; an argument that names none is the same for every part. Nothing has to cross between parts.
Inputs may be any that keep to these rules, and one draw needn't show every extreme that they name: `adapter_ranks`: each rank is 128, 64, 32 or 16; some adapter has rank 128.
All inputs are finite; a program needn't handle non-finite values.
Results may differ from a plain program's by a relative error of at most 0.013.
Values may be sent and summed in bfloat16 or wider, within the bound.
No kernel may reach another device: no remote copies, remote signals or barrier semaphores. Data moves between devices by JAX's collectives and lax.ppermute only.
A program may use at most 192 MiB of HBM per device.

v0:
```python
import jax
import jax.numpy as jnp
from jax import lax
from jax.sharding import PartitionSpec as P


def per_device(
    hidden_activations,
    down_matrix,
    adapter_input_factor,
    adapter_output_factor,
    token_requests,
    request_adapters,
    adapter_ranks,
    adapter_store_slot,
):
    store_shard_index = lax.axis_index("store")
    token_rows = hidden_activations.shape[0]
    request_list = request_adapters.shape[0]
    held_slot_count = adapter_input_factor.shape[0]
    rank_padded_width = adapter_input_factor.shape[2]
    rank_row_mask = adapter_output_factor.shape[1]
    token_window = 2 * token_rows // request_list
    adapter_ids = jnp.arange(adapter_ranks.shape[0], dtype=jnp.int32)
    lookup_table = request_adapters[:, None] == adapter_ids[None, :]
    request_adapter_rank = jnp.sum(jnp.where(lookup_table, adapter_ranks[None, :], 0), axis=1)
    request_store_slot = jnp.sum(jnp.where(lookup_table, adapter_store_slot[None, :], 0), axis=1)
    owning_shard = request_store_slot // held_slot_count
    shard_local_slot = request_store_slot % held_slot_count
    adapter_scale = 0.25 * rank_padded_width / request_adapter_rank.astype(jnp.float32)
    request_numbers = jnp.arange(request_list, dtype=jnp.int32)
    first_token = jnp.sum(
        (token_requests[None, :] < request_numbers[:, None]).astype(jnp.int32), axis=1
    )
    window_start = jnp.minimum(first_token, token_rows - token_window)
    columns = jnp.arange(rank_padded_width, dtype=jnp.int32)

    def accumulate_request(adapter_partial, request_number, adapter_row_block):
        first_row = window_start[request_number]
        window_rows = lax.dynamic_slice_in_dim(hidden_activations, first_row, token_window, 0)
        product = jnp.dot(window_rows, adapter_row_block, preferred_element_type=jnp.float32)
        window_ids = lax.dynamic_slice_in_dim(token_requests, first_row, token_window, 0)
        keep_mask = (window_ids == request_number)[:, None] & (
            columns < request_adapter_rank[request_number]
        )[None, :]
        current_output = lax.dynamic_slice_in_dim(adapter_partial, first_row, token_window, 0)
        updated_output = current_output + jnp.where(keep_mask, product, 0.0)
        return lax.dynamic_update_slice_in_dim(adapter_partial, updated_output, first_row, 0)

    empty_adapter_product = jnp.zeros((token_rows, rank_padded_width), jnp.float32)

    def process_request(request_number, adapter_partial):

        def compute_output(partial_input):
            adapter_row_block = lax.dynamic_index_in_dim(
                adapter_input_factor, shard_local_slot[request_number], 0, keepdims=False
            )
            return accumulate_request(partial_input, request_number, adapter_row_block)

        return lax.cond(
            owning_shard[request_number] == store_shard_index,
            compute_output,
            lambda partial_input: partial_input,
            adapter_partial,
        )

    adapter_partial = lax.fori_loop(0, request_list, process_request, empty_adapter_product)
    summed_cols = lax.psum_scatter(
        adapter_partial.astype(jnp.bfloat16), "tensor", scatter_dimension=1, tiled=True
    )
    adapter_block_term = lax.psum(summed_cols, "store").astype(jnp.float32)
    selected_output_factor = jnp.take(adapter_output_factor, shard_local_slot, axis=0)
    offered = jnp.where(
        (owning_shard == store_shard_index)[:, None, None],
        selected_output_factor,
        jnp.zeros_like(selected_output_factor),
    )
    b_columns = lax.psum_scatter(offered, "store", scatter_dimension=2, tiled=True).astype(
        jnp.float32
    )
    b_stack = b_columns.reshape(request_list * rank_row_mask, b_columns.shape[2])
    weight_matrices = jnp.where(
        token_requests[:, None] == request_numbers[None, :], adapter_scale[None, :], 0.0
    )
    expanded_rows = (weight_matrices[:, :, None] * adapter_block_term[:, None, :]).reshape(
        token_rows, request_list * rank_row_mask
    )
    base_product = jnp.dot(hidden_activations, down_matrix, preferred_element_type=jnp.float32)
    adapter_product = jnp.dot(
        expanded_rows, b_stack, precision=lax.Precision.HIGHEST, preferred_element_type=jnp.float32
    )
    return lax.psum_scatter(
        (base_product + adapter_product).astype(jnp.bfloat16),
        "tensor",
        scatter_dimension=0,
        tiled=True,
    )


def solution(mesh):
    in_specs = (
        P("groups", "tensor"),
        P("tensor", "store"),
        P(("groups", "store"), "tensor", None),
        P(("groups", "store"), "tensor", None),
        P("groups"),
        P("groups"),
        P("groups"),
        P("groups"),
    )
    out_specs = P(("groups", "tensor"), "store")
    return jax.shard_map(
        per_device, mesh=mesh, in_specs=in_specs, out_specs=out_specs, check_vma=False
    )
```

profile of v0, /device:TPU:0, one launch (start us, length us, event | category | flops | bytes accessed | tf_op | source)
XLA Modules:
  0.0 222.6 jit_solution(16212647780802485594)
XLA Ops:
  6.5 1.0 convert_reduce_fusion
  7.5 0.9 select_reduce_fusion.1
  8.5 34.0 %while.17 = (s32[]{:T(128)}, f32[1024,128]{1,0:T(8,128)S(1)}, s32[4]{0:T(128)S(1)}, s32[]{:T(128)}, s32[4]{0:T(128)S(1)}, /*index=5*/s32[1024]{0:T(1024)}, s32[4...) while((s32[]{:T(128)}, f32[1024,128]{1,0:T(8,128)S(1)}, ...), condition=%wide.region_6.7_spmd.clone, body=%wide.region_3.6_spmd.clone.sunk | while | flops 939721344 | bytes 10229881 | solution.py:67
  8.5 0.6 dynamic_slice.47
  9.8 14.9 %conditional.3 = (f32[1024,128]{1,0:T(8,128)S(1)}) conditional(s32[]{:T(128)} %convert_element_type.37, f32[1024,128]{1,0:T(8,128)S(1)} %get-tuple-element.348, (s32[]{:T(128)}, s32[4]{0:T(128)S(1)}, f32[1024,128]{1,0:T(8,128)S(1)}, s32[1024]{0:T(1024)}, s32[4]{0:T(128)S(1)}, /*index=5*/s32[128]{0:T(128)S(1)}, bf16[1024,7168]{1,0:T(8,128)(2,1)}, ...), branch_computations={%region_4.4_spmd, %region_5.5_spmd} | conditional | flops 939721344 | bytes 10229154 | solution.py:60
  9.8 0.7 dynamic_slice.26
  12.3 0.7 dynamic_slice.24
  13.0 0.6 broadcast_compare_fusion
  13.6 0.7 dynamic_slice.21
  16.2 0.8 dynamic-slice_compare_fusion
  16.9 5.7 %fusion.11 = f32[512,128]{1,0:T(8,128)S(1)} fusion(bf16[4,7168,128]{2,1,0:T(8,128)(2,1)} %get-tuple-element.209, s32[]{:T(128)S(6)} %select_n.77, bf16[1024,7168]{1,0:T(8,128)(2,1)} %get-tuple-element.208, s32[]{:T(128)S(6)} %select_n.76, f32[1024,128]{1,0:T(8,128)S(1)} %get-tuple-element.202, pred[128]{0:T(512)(128)(4,1)S(1)} %broadcast_compare_fusion, ...), kind=kOutput, calls=%fused_computation.7 | convolution fusion | flops 939720704 | bytes 9701504 | tf_op jit(solution)/shard_map/while/body/eval_jaxpr/cond/branch_1_fun/dot_general | solution.py:41
  22.7 1.9 dynamic_update_slice.2
  24.6 0.6 dynamic_slice.47
  25.9 0.6 dynamic_slice.47
  27.2 0.6 dynamic_slice.47
  28.5 14.0 %conditional.3 = (f32[1024,128]{1,0:T(8,128)S(1)}) conditional(s32[]{:T(128)} %convert_element_type.37, f32[1024,128]{1,0:T(8,128)S(1)} %get-tuple-element.348, (s32[]{:T(128)}, s32[4]{0:T(128)S(1)}, f32[1024,128]{1,0:T(8,128)S(1)}, s32[1024]{0:T(1024)}, s32[4]{0:T(128)S(1)}, /*index=5*/s32[128]{0:T(128)S(1)}, bf16[1024,7168]{1,0:T(8,128)(2,1)}, ...), branch_computations={%region_4.4_spmd, %region_5.5_spmd} | conditional | flops 939721344 | bytes 10229154 | solution.py:60
  28.5 0.7 dynamic_slice.26
  31.1 0.7 dynamic_slice.24
  31.7 0.6 broadcast_compare_fusion
  32.4 0.7 dynamic_slice.21
  34.9 0.8 dynamic-slice_compare_fusion
  35.7 5.7 %fusion.11 = f32[512,128]{1,0:T(8,128)S(1)} fusion(bf16[4,7168,128]{2,1,0:T(8,128)(2,1)} %get-tuple-element.209, s32[]{:T(128)S(6)} %select_n.77, bf16[1024,7168]{1,0:T(8,128)(2,1)} %get-tuple-element.208, s32[]{:T(128)S(6)} %select_n.76, f32[1024,128]{1,0:T(8,128)S(1)} %get-tuple-element.202, pred[128]{0:T(512)(128)(4,1)S(1)} %broadcast_compare_fusion, ...), kind=kOutput, calls=%fused_computation.7 | convolution fusion | flops 939720704 | bytes 9701504 | tf_op jit(solution)/shard_map/while/body/eval_jaxpr/cond/branch_1_fun/dot_general | solution.py:41
  41.4 1.1 dynamic_update_slice.2
  42.5 0.9 copy.13
  43.5 2.1 gather_fusion
  45.6 20.3 %reduce-scatter.10.cloned.1.call-done = bf16[32,1024]{1,0:T(8,128)(2,1)} async-done(((bf16[128,1024]{1,0:T(8,128)(2,1)}), bf16[32,1024]{1,0:T(8,128)(2,1)}) %reduce-scatter.10.cloned.1.call-update) | async-done | bytes 65552
  66.0 3.3 %select_select_fusion = bf16[4,32,8192]{2,1,0:T(8,128)(2,1)} fusion(bf16[4,32,8192]{2,1,0:T(8,128)(2,1)} %gather_fusion, pred[4]{0:T(512)(128)(4,1)S(1)} %get-tuple-element.273, pred[4]{0:T(512)(128)(4,1)S(1)} %get-tuple-element.269), kind=kLoop, calls=%fused_computation.13 | loop fusion | flops 2097152 | bytes 4194312 | tf_op jit(solution)/shard_map/jit(_where)/select_n | solution.py:73
  69.4 38.4 %fusion.24 = f32[1024,2048]{1,0:T(8,128)} fusion(bf16[1024,7168]{1,0:T(8,128)(2,1)} %get-tuple-element.386, bf16[7168,2048]{1,0:T(8,128)(2,1)} %param.13), kind=kOutput, calls=%fused_computation.41 | convolution fusion | flops 30064771072 | bytes 52428800 | tf_op jit(solution)/shard_map/dot_general | solution.py:88
  107.8 1.0 convert_element_type.30
  108.8 22.8 %reduce-scatter.6.cloned.1.call-done = bf16[4,32,2048]{2,1,0:T(8,128)(2,1)} async-done(((bf16[4,32,8192]{2,1,0:T(8,128)(2,1)}), bf16[4,32,2048]{2,1,0:T(8,128)(2,1)}) %reduce-scatter.6.cloned.1.call-update) | async-done | bytes 524304 | tf_op jit(solution)/shard_map/reduce_scatter | solution.py:78
  131.7 7.5 %fusion.17 = bf16[1024,2048]{1,0:T(8,128)(2,1)} fusion(f32[1024,2048]{1,0:T(8,128)} %fusion.24, bf16[4,32,2048]{2,1,0:T(8,128)(2,1)} %reduce-scatter.6.cloned.1.call-done, f32[1024,32]{0,1:T(8,128)S(1)} %convert_element_type.30, f32[1024,4]{0,1:T(4,128)S(1)} %fusion.21), kind=kOutput, calls=%fused_computation.12 | convolution fusion | flops 3225550848 | bytes 13254656 | tf_op jit(solution)/shard_map/dot_general | solution.py:89
  139.2 76.9 %reduce-scatter.8.cloned.1.call-done = bf16[256,2048]{1,0:T(8,128)(2,1)} async-done(((bf16[1024,2048]{1,0:T(8,128)(2,1)}), bf16[256,2048]{1,0:T(8,128)(2,1)}) %reduce-scatter.8.cloned.1.call-update) | async-done | bytes 1048592 | tf_op jit(solution)/shard_map/reduce_scatter | solution.py:92
  (29 shorter events, 0.4 us)
Async XLA Ops:
  6.5 37.0 %copy-start = (bf16[4,32,8192]{2,1,0:T(8,128)(2,1)S(1)}, bf16[4,32,8192]{2,1,0:T(8,128)(2,1)}, u32[]{:S(2)}) copy-start(bf16[4,32,8192]{2,1,0:T(8,128)(2,1)} %param.15) | copy-start | bytes 6291460
  6.5 59.4 %reduce-scatter.10.cloned.1.call-start = ((), (), s32[]{:S(2)}) async-start(), calls=%async_computation.6 | async-start | bytes 327680
  42.5 26.9 %copy-start.2 = (s32[1024]{0:T(1024)S(1)}, s32[1024]{0:T(1024)}, u32[]{:S(2)}) copy-start(s32[1024]{0:T(1024)} %get-tuple-element.380) | copy-start | bytes 12292
  43.4 64.4 %all-reduce.2.cloned.1.call-start = ((), (), s32[]{:S(2)}) async-start(), calls=%async_computation.3 | async-start | bytes 131072 | tf_op jit(solution)/shard_map/psum | solution.py:71
  65.9 65.7 %reduce-scatter.6.cloned.1.call-start = ((), (), s32[]{:S(2)}) async-start(), calls=%async_computation.4 | async-start | bytes 2621440 | tf_op jit(solution)/shard_map/reduce_scatter | solution.py:78
  69.3 146.8 %reduce-scatter.8.cloned.1.call-start = ((), (), s32[]{:S(2)}) async-start(), calls=%async_computation.5 | async-start | bytes 5242880 | tf_op jit(solution)/shard_map/reduce_scatter | solution.py:92
  107.8 108.3 %copy-start.1 = (bf16[4,32,8192]{2,1,0:T(8,128)(2,1)S(1)}, bf16[4,32,8192]{2,1,0:T(8,128)(2,1)}, u32[]{:S(2)}) copy-start(bf16[4,32,8192]{2,1,0:T(8,128)(2,1)} %param.15) | copy-start | bytes 6291460
Sparse Core Ops, SparseCore 0:
  43.5 22.3 reduce-scatter.9
  68.3 29.2 all-reduce.1
  100.2 31.4 reduce-scatter.5
  139.3 76.7 reduce-scatter.7
where the time goes:
time: 222 us; the launch traced here: 223 us
  waiting for transfers between devices  120 us (54%)
  matrix products  57.3 us (26%)
  between operations  13.2 us (6%)
  local copies, waits for them, and re-layouts  12.4 us (6%)
  loops' own time  10.4 us (5%)
  other arithmetic  9.1 us (4%)
    reduce_scatter x1, waiting for transfers between devices, per_device(): lax.psum_scatter((base_product + adapter_product).astype(jnp.bfloat16), '...  76.9 us
    dot_general x1, matrix products, per_device(): jnp.dot(hidden_activations, down_matrix, preferred_element_type=jnp.float32)  38.4 us
    reduce_scatter x1, waiting for transfers between devices, per_device(): lax.psum_scatter(offered, 'store', scatter_dimension=2, tiled=True)  22.8 us
    unnamed x5, waiting for transfers between devices  20.4 us
    dot_general x2, matrix products, accumulate_request(): jnp.dot(window_rows, adapter_row_block, preferred_element_type=jnp.float32)  11.4 us
    another operation x4, loops' own time, process_request(): lax.cond(owning_shard[request_number] == store_shard_index, compute_outpu...  7.72 us
    dot_general x1, matrix products, per_device(): jnp.dot(expanded_rows, b_stack, precision=lax.Precision.HIGHEST, preferre...  7.51 us
  transfers between devices with their start and end apart: 4, of which 3 were waited for; matrix products, arithmetic and copies ran while one was open for 20% of the time, Pallas kernels for 0%

commit v1 on v0

v1 whole, which is shorter than its diff:
```python
import functools

import jax
import jax.numpy as jnp
import numpy as np
from jax import lax
from jax.experimental import pallas as pl
from jax.experimental.pallas import tpu as pltpu
from jax.sharding import PartitionSpec as P

CHUNKS = 4


def line_order(n):
    order = []
    for z in range(n):
        sends = [(t, z >= n // 2, n - 1 - t + z) for t in range(z, n - 1)]
        sends += [(t, z < n // 2, t - (n - 1 - z)) for t in range(n - 1 - z, n - 1)]
        order.append([block for _, _, block in sorted(sends)] + [z])
    return order


def first_divisor(size, choices):
    for choice in choices:
        if size % choice == 0:
            return choice
    return size


def adapter_input_kernel(
    shard_ref, request_adapters_ref, ranks_ref, slots_ref, requests_ref, hidden_ref, factor_ref, out_ref, sums_ref
):
    step = pl.program_id(0)
    held, _, width = factor_ref.shape
    factors = jnp.concatenate([factor_ref[s] for s in range(held)], axis=1)
    product = jnp.dot(hidden_ref[...], factors, preferred_element_type=jnp.float32)

    @pl.when(step == 0)
    def _():
        for s in range(held):
            sums_ref[s] = product[:, s * width : (s + 1) * width]

    @pl.when(step > 0)
    def _():
        for s in range(held):
            sums_ref[s] += product[:, s * width : (s + 1) * width]

    @pl.when(step == pl.num_programs(0) - 1)
    def _():
        requests = requests_ref[...]
        row = lax.broadcasted_iota(jnp.int32, out_ref.shape, 0)
        column = lax.broadcasted_iota(jnp.int32, out_ref.shape, 1)
        total = jnp.zeros(out_ref.shape, jnp.float32)
        for r in range(request_adapters_ref.shape[0]):
            adapter = request_adapters_ref[r]
            local_slot = slots_ref[adapter] - shard_ref[0] * held
            owned = (local_slot >= 0) & (local_slot < held)
            start = jnp.sum((requests < r).astype(jnp.int32))
            end = jnp.where(owned, jnp.sum((requests <= r).astype(jnp.int32)), 0)
            keep = (row >= start) & (row < end) & (column < ranks_ref[adapter])
            total = jnp.where(keep, sums_ref[jnp.clip(local_slot, 0, held - 1)], total)
        out_ref[...] = total.astype(out_ref.dtype)


def adapter_input(hidden, factor, token_requests, request_adapters, ranks, slots, shard):
    tokens, depth = hidden.shape
    held, _, width = factor.shape
    tile = first_divisor(depth, (1024, 896, 512, 256, 128))
    smem = pl.BlockSpec(memory_space=pltpu.SMEM)
    return pl.pallas_call(
        adapter_input_kernel,
        out_shape=jax.ShapeDtypeStruct((tokens, width), jnp.bfloat16),
        grid=(depth // tile,),
        in_specs=[
            smem,
            smem,
            smem,
            smem,
            pl.BlockSpec((tokens // 128, 128), lambda k: (0, 0)),
            pl.BlockSpec((tokens, tile), lambda k: (0, k)),
            pl.BlockSpec((held, tile, width), lambda k: (0, k, 0)),
        ],
        out_specs=pl.BlockSpec((tokens, width), lambda k: (0, 0)),
        scratch_shapes=[pltpu.VMEM((held, tokens, width), jnp.float32)],
        compiler_params=pltpu.CompilerParams(vmem_limit_bytes=24 * 1024 * 1024),
        cost_estimate=pl.CostEstimate(
            flops=2 * tokens * depth * held * width,
            bytes_accessed=2 * depth * (tokens + held * width),
            transcendentals=0,
        ),
        name="adapter_input",
    )(shard[None], request_adapters, ranks, slots, token_requests.reshape(tokens // 128, 128), hidden, factor)


def swap(x, axis, bit):
    return lax.ppermute(x, axis, [(i, i ^ bit) for i in range(lax.axis_size(axis))])


def bits_of(size):
    return [1 << i for i in range(size.bit_length() - 1)]


def sum_to_shards(x, axis, dim):
    me = lax.axis_index(axis)
    for bit in bits_of(lax.axis_size(axis)):
        shape = x.shape
        x = x.reshape(shape[:dim] + (shape[dim] // 2, 2) + shape[dim + 1 :])
        side = (me // bit) % 2
        kept = lax.dynamic_index_in_dim(x, side, dim + 1, keepdims=False)
        sent = lax.dynamic_index_in_dim(x, 1 - side, dim + 1, keepdims=False)
        x = kept + swap(sent, axis, bit)
    return lax.squeeze(x, (dim,))


def gather_shards(x, axis, dim):
    me = lax.axis_index(axis)
    x = jnp.expand_dims(x, dim)
    for bit in reversed(bits_of(lax.axis_size(axis))):
        other = swap(x, axis, bit)
        high = (me // bit) % 2 == 1
        pair = jnp.where(high, jnp.stack([other, x], dim + 1), jnp.stack([x, other], dim + 1))
        x = pair.reshape(pair.shape[:dim] + (-1,) + pair.shape[dim + 2 :])
    return x


def sum_to_blocks(x, axis):
    n = lax.axis_size(axis)
    me = lax.axis_index(axis)
    total = lax.dynamic_index_in_dim(x, me, 0, keepdims=False).astype(jnp.float32)
    for shift in range(1, n):
        sent = lax.dynamic_index_in_dim(x, (me + shift) % n, 0, keepdims=False)
        total += lax.ppermute(sent, axis, [(i, (i + shift) % n) for i in range(n)]).astype(jnp.float32)
    return total.astype(x.dtype)


def gather_along_line(x, axis):
    n = lax.axis_size(axis)
    up, down = [x], [x]
    for j in range(1, n):
        up.append(lax.ppermute(up[-1], axis, [(i, i + 1) for i in range(j - 1, n - 1)]))
        down.append(lax.ppermute(down[-1], axis, [(i, i - 1) for i in range(n - j, 0, -1)]))
    return [x] + [up[j] + down[n - j] for j in range(1, n)]


def per_device(
    hidden_activations,
    down_matrix,
    adapter_input_factor,
    adapter_output_factor,
    token_requests,
    request_adapters,
    adapter_ranks,
    adapter_store_slot,
):
    n = lax.axis_size("tensor")
    place = lax.axis_index("tensor")
    shards = lax.axis_size("store")
    shard = lax.axis_index("store")
    tokens = hidden_activations.shape[0]
    block = tokens // n
    held, rank_rows, model_width = adapter_output_factor.shape
    width = down_matrix.shape[1]
    requests = request_adapters.shape[0]
    order = line_order(n)
    my_blocks = jnp.asarray(np.array(order, np.int32))[place]

    def slot_rows(s):
        return lax.dynamic_slice_in_dim(hidden_activations, my_blocks[s] * block, block, 0)

    def base_terms(matrix):
        return [
            lax.optimization_barrier(
                jnp.dot(slot_rows(s), matrix, preferred_element_type=jnp.float32).astype(jnp.bfloat16)
            )
            for s in range(n)
        ]

    chunk = width // CHUNKS
    first = base_terms(down_matrix[:, :chunk])
    later_matrix, factor, _ = lax.optimization_barrier((down_matrix, adapter_input_factor, first[n - 2]))

    partial = adapter_input(
        hidden_activations, factor, token_requests, request_adapters, adapter_ranks, adapter_store_slot, shard
    )
    later_matrix, partial = lax.optimization_barrier((later_matrix, partial))
    piece = tokens // (n * shards)
    pieces = sum_to_shards(partial.reshape(n, shards, piece, -1), "store", 1)
    lora = gather_shards(sum_to_blocks(pieces, "tensor"), "store", 0).reshape(block, -1)

    slot_of = adapter_store_slot[request_adapters]
    rank_of = adapter_ranks[request_adapters]
    offered = jnp.where(
        (slot_of // held == shard)[:, None, None], adapter_output_factor[slot_of % held], jnp.bfloat16(0)
    )
    rows = sum_to_shards(offered.reshape(requests * rank_rows, shards, width), "store", 1)
    rows = jnp.concatenate(gather_along_line(rows, "tensor"), axis=0)

    scale = 0.25 * lora.shape[1] / rank_of.astype(jnp.float32)
    my_requests = lax.dynamic_slice_in_dim(token_requests, place * block, block, 0)
    weights = jnp.where(my_requests[:, None] == jnp.arange(requests)[None, :], scale[None, :], 0.0)
    expanded = jnp.concatenate(
        [
            (
                weights[:, :, None]
                * lax.dynamic_slice_in_dim(lora, (place - j) % n * rank_rows, rank_rows, 1)[:, None, :]
            ).reshape(block, requests * rank_rows)
            for j in range(n)
        ],
        axis=1,
    ).astype(jnp.bfloat16)

    outputs = []
    for c in range(CHUNKS):
        columns = slice(c * chunk, (c + 1) * chunk)
        terms = first if c == 0 else base_terms(later_matrix[:, columns])
        arrived = {}
        for t in range(n - 1):
            for j in range(t + 1):
                sent = terms[order[j].index(n - 1 - t + j)]
                if j > 0:
                    sent = sent.astype(jnp.float32) + arrived[j - 1, t - 1].astype(jnp.float32)
                arrived[j, t] = lax.ppermute(
                    sent.astype(jnp.bfloat16), "tensor", [(j, j + 1), (n - 1 - j, n - 2 - j)]
                )
        total = jnp.dot(expanded, rows[:, columns], preferred_element_type=jnp.float32)
        total = lax.optimization_barrier(total + terms[n - 1].astype(jnp.float32))
        for j in range(n - 1):
            total += arrived[j, n - 2].astype(jnp.float32)
        outputs.append(total.astype(jnp.bfloat16))
    return jnp.concatenate(outputs, axis=1)


def solution(mesh):
    in_specs = (
        P("groups", "tensor"),
        P("tensor", "store"),
        P(("groups", "store"), "tensor", None),
        P(("groups", "store"), "tensor", None),
        P("groups"),
        P("groups"),
        P("groups"),
        P("groups"),
    )
    out_specs = P(("groups", "tensor"), "store")
    return jax.shard_map(
        per_device, mesh=mesh, in_specs=in_specs, out_specs=out_specs, check_vma=False
    )
```

time: 222 us -> 295 us (1.33); the launches traced: 223 us -> 289 us
  waiting for transfers between devices: 120 us -> 37.3 us
  starting transfers between devices: 0.12 us -> 80.4 us
  matrix products: 57.3 us -> 104 us
  other arithmetic: 9.1 us -> 24.9 us
  local copies, waits for them, and re-layouts: 12.4 us -> 25.9 us
  Pallas kernels: 0 us -> 13.3 us
  loops' own time: 10.4 us -> 0 us
  between operations: 13.2 us -> 3.57 us
    reduce_scatter x2 -> x0, waiting for transfers between devices: 99.8 us -> none  [the longest x1 76.9 us: per_device(): lax.psum_scatter((base_product + adapter_product).astype(jnp.bfloat16), '...]
    ppermute x0 -> x39, starting transfers between devices: none -> 80.4 us  [the longest x24 63.1 us: per_device(): lax.ppermute(sent.astype(jnp.bfloat16), 'tensor', [(j, j + 1), (n - 1 - j...]
    dot_general x4 -> x20, matrix products: 57.3 us -> 104 us  [the longest x16 103 us: base_terms(): jnp.dot(slot_rows(s), matrix, preferred_element_type=jnp.float32)]
    ppermute x0 -> x39, waiting for transfers between devices: none -> 37.3 us  [the longest x24 16.9 us: per_device(): lax.ppermute(sent.astype(jnp.bfloat16), 'tensor', [(j, j + 1), (n - 1 - j...]
    unnamed x5 -> x0, waiting for transfers between devices: 20.4 us -> none
    convert_element_type x2 -> x21, other arithmetic: 1.03 us -> 16.9 us  [the longest x12 14.6 us: per_device(): sent.astype(jnp.bfloat16)]
    pallas_call x0 -> x1, Pallas kernels: none -> 13.3 us  [adapter_input(): pl.pallas_call(adapter_input_kernel, out_shape=jax.ShapeDtypeStruct((toke...]
    another operation x5 -> x0, loops' own time: 10.4 us -> none  [the longest x4 7.72 us: process_request(): lax.cond(owning_shard[request_number] == store_shard_index, compute_outpu...]
  transfers between devices with their start and end apart: 4 -> 39, of which waited for: 3 -> 11; matrix products, arithmetic and copies ran while one was open for 20% -> 47% of each run, Pallas kernels for 0% -> 5%
where the time goes in v1:
time: 295 us; the launch traced here: 289 us
  matrix products  104 us (35%)
  starting transfers between devices  80.4 us (27%)
  waiting for transfers between devices  37.3 us (13%)
  local copies, waits for them, and re-layouts  25.9 us (9%)
  other arithmetic  24.9 us (8%)
  Pallas kernels  13.3 us (5%)
  between operations  3.57 us (1%)
    dot_general x16, matrix products, base_terms(): jnp.dot(slot_rows(s), matrix, preferred_element_type=jnp.float32)  103 us
    ppermute x24, starting transfers between devices, per_device(): lax.ppermute(sent.astype(jnp.bfloat16), 'tensor', [(j, j + 1), (n - 1 - j...  63.1 us
    ppermute x24, waiting for transfers between devices, per_device(): lax.ppermute(sent.astype(jnp.bfloat16), 'tensor', [(j, j + 1), (n - 1 - j...  16.9 us
    convert_element_type x12, other arithmetic, per_device(): sent.astype(jnp.bfloat16)  14.6 us
    pallas_call x1, Pallas kernels, adapter_input(): pl.pallas_call(adapter_input_kernel, out_shape=jax.ShapeDtypeStruct((toke...  13.3 us
    ppermute x3, waiting for transfers between devices, gather_along_line(): lax.ppermute(down[-1], axis, [(i, i - 1) for i in range(n - j, 0, -1)])  12.8 us
    unnamed x64, local copies, waits for them, and re-layouts  9.27 us
    dynamic_slice x1, local copies, waits for them, and re-layouts, sum_to_shards(): kept = lax.dynamic_index_in_dim(x, side, dim + 1, keepdims=False)  6.18 us
  transfers between devices with their start and end apart: 39, of which 11 were waited for; matrix products, arithmetic and copies ran while one was open for 47% of the time, Pallas kernels for 5%

profile of v1, /device:TPU:0, one launch (start us, length us, event | category | flops | bytes accessed | tf_op | source)
XLA Modules:
  0.0 289.2 jit_solution(1430663172692231547)
XLA Ops:
  2.2 7.0 %fusion.48 = bf16[256,512]{1,0:T(8,128)(2,1)} fusion(bf16[7168,2048]{1,0:T(8,128)(2,1)} %param.10, bf16[1024,7168]{1,0:T(8,128)(2,1)} %hidden_ref.1, s32[]{:T(128)S(6)} %select_n.221), kind=kOutput, calls=%fused_computation.57 | convolution fusion | flops 1879179264 | bytes 11272196 | tf_op jit(solution)/shard_map/dot_general | solution.py:173
  9.2 5.6 %collective-permute-start.15 = (bf16[256,512]{1,0:T(8,128)(2,1)}, bf16[256,512]{1,0:T(8,128)(2,1)}, u32[]{:S(2)}, u32[]{:S(2)}) collective-permute-start(bf16[256,512]{1,0:T(8,128)(2,1)} %fusion.48), channel_id=1, source_target_pairs={{0,4},{12,8},{1,5},{13,9},{2,6},{14,10},{3,7},{15,11},{16,20},{28,... | collective-permute-start | bytes 786440 | tf_op jit(solution)/shard_map/ppermute | solution.py:222
  14.9 5.2 %copy-done.5 = bf16[1024,7168]{1,0:T(8,128)(2,1)S(1)} copy-done((bf16[1024,7168]{1,0:T(8,128)(2,1)S(1)}, bf16[1024,7168]{1,0:T(8,128)(2,1)}, u32[]{:S(2)}) %copy-start.5) | copy-done | bytes 14680088
  23.1 13.3 %adapter_input.1 = bf16[1024,128]{1,0:T(8,128)(2,1)S(1)} custom-call(s32[1]{0:T(128)} %bitcast.1.shard_ref, s32[4]{0:T(128)S(1)} %copy-done.7, s32[16]{0:T(128)S(1)} %copy-done.3, s32[16]{0:T(128)S(1)} %copy-done.2, s32[8,128]{1,0:T(8,128)S(1)} %bitcast.42, bf16[1024,7168]{1,0:T(8,128)(2,1)S(1)} %copy-done.5, bf16[4,7168,128]{2,1,0:T(8,128)(2,1)S(1)} %copy-done.6), custom_call_target="tpu_custom_call" | custom-call | flops 7516192768 | bytes 22020096 | tf_op jit(solution)/shard_map/adapter_input/pallas_call | solution.py:70
  39.4 3.5 %gather.17 = bf16[128,2,2,2048]{3,2,1,0:T(2,128)(2,1)S(1)} reshape(bf16[4,32,8192]{2,1,0:T(8,128)(2,1)} %gather_fusion.2) | data formatting | bytes 4194304 | tf_op jit(solution)/shard_map/gather | solution.py:193
  44.8 6.2 %constant_dynamic-slice_fusion.2 = (bf16[128,2,1,2048]{3,2,1,0:T(2,128)(2,1)}, bf16[128,2,1,2048]{3,2,1,0:T(2,128)(2,1)S(1)}) fusion(bf16[128,2,2,2048]{3,2,1,0:T(2,128)(2,1)S(1)} %broadcast_select_fusion, s32[]{:T(128)S(6)} %select_n.222, s32[]{:T(128)S(6)} %select_n.223), kind=kLoop, calls=%fused_computation.132 | loop fusion | bytes 4194312 | tf_op jit(solution)/shard_map/jit(dynamic_index_in_dim)/dynamic_slice | solution.py:109
  54.4 7.0 %fusion.53 = bf16[256,512]{1,0:T(8,128)(2,1)} fusion(bf16[7168,2048]{1,0:T(8,128)(2,1)} %param.10, bf16[1024,7168]{1,0:T(8,128)(2,1)} %hidden_ref.1, s32[]{:T(128)S(6)} %select_n.249), kind=kOutput, calls=%fused_computation.58 | convolution fusion | flops 1879179264 | bytes 11272196 | tf_op jit(solution)/shard_map/dot_general | solution.py:173
  61.4 7.1 %fusion.63 = bf16[256,512]{1,0:T(8,128)(2,1)} fusion(bf16[7168,2048]{1,0:T(8,128)(2,1)} %param.10, bf16[1024,7168]{1,0:T(8,128)(2,1)} %hidden_ref.1, s32[]{:T(128)S(6)} %select_n.251), kind=kOutput, calls=%fused_computation.60 | convolution fusion | flops 1879179264 | bytes 11272196 | tf_op jit(solution)/shard_map/dot_general | solution.py:173
  68.5 7.1 %fusion.68 = bf16[256,512]{1,0:T(8,128)(2,1)} fusion(bf16[7168,2048]{1,0:T(8,128)(2,1)} %param.10, bf16[1024,7168]{1,0:T(8,128)(2,1)} %hidden_ref.1, s32[]{:T(128)S(6)} %select_n.249), kind=kOutput, calls=%fused_computation.61 | convolution fusion | flops 1879179264 | bytes 11272196 | tf_op jit(solution)/shard_map/dot_general | solution.py:173
  75.6 6.3 %fusion.83 = bf16[256,512]{1,0:T(8,128)(2,1)} fusion(bf16[7168,2048]{1,0:T(8,128)(2,1)} %param.10, bf16[1024,7168]{1,0:T(8,128)(2,1)S(1)} %bitcast.44, s32[]{:T(128)S(6)} %select_n.251), kind=kOutput, calls=%fused_computation.64 | convolution fusion | flops 1879179264 | bytes 11272196 | tf_op jit(solution)/shard_map/dot_general | solution.py:173
  81.9 5.8 %fusion.73 = bf16[256,512]{1,0:T(8,128)(2,1)} fusion(bf16[7168,2048]{1,0:T(8,128)(2,1)} %param.10, bf16[1024,7168]{1,0:T(8,128)(2,1)S(1)} %bitcast.44, s32[]{:T(128)S(6)} %select_n.221), kind=kOutput, calls=%fused_computation.62 | convolution fusion | flops 1879179264 | bytes 11272196 | tf_op jit(solution)/shard_map/dot_general | solution.py:173
  87.7 7.1 %fusion.58 = bf16[256,512]{1,0:T(8,128)(2,1)} fusion(bf16[7168,2048]{1,0:T(8,128)(2,1)} %param.10, bf16[1024,7168]{1,0:T(8,128)(2,1)} %hidden_ref.1, s32[]{:T(128)S(6)} %select_n.250), kind=kOutput, calls=%fused_computation.59 | convolution fusion | flops 1879179264 | bytes 11272196 | tf_op jit(solution)/shard_map/dot_general | solution.py:173
  94.8 7.1 %fusion.78 = bf16[256,512]{1,0:T(8,128)(2,1)} fusion(bf16[7168,2048]{1,0:T(8,128)(2,1)} %param.10, bf16[1024,7168]{1,0:T(8,128)(2,1)} %hidden_ref.1, s32[]{:T(128)S(6)} %select_n.250), kind=kOutput, calls=%fused_computation.63 | convolution fusion | flops 1879179264 | bytes 11272196 | tf_op jit(solution)/shard_map/dot_general | solution.py:173
  101.9 5.9 %fusion.88 = bf16[256,512]{1,0:T(8,128)(2,1)} fusion(bf16[7168,2048]{1,0:T(8,128)(2,1)} %param.10, bf16[1024,7168]{1,0:T(8,128)(2,1)S(1)} %bitcast.46, s32[]{:T(128)S(6)} %select_n.249), kind=kOutput, calls=%fused_computation.65 | convolution fusion | flops 1879179264 | bytes 11272196 | tf_op jit(solution)/shard_map/dot_general | solution.py:173
  107.8 5.9 %fusion.103 = bf16[256,512]{1,0:T(8,128)(2,1)} fusion(bf16[7168,2048]{1,0:T(8,128)(2,1)} %param.10, bf16[1024,7168]{1,0:T(8,128)(2,1)S(1)} %bitcast.46, s32[]{:T(128)S(6)} %select_n.251), kind=kOutput, calls=%fused_computation.68 | convolution fusion | flops 1879179264 | bytes 11272196 | tf_op jit(solution)/shard_map/dot_general | solution.py:173
  113.7 5.9 %fusion.93 = bf16[256,512]{1,0:T(8,128)(2,1)} fusion(bf16[7168,2048]{1,0:T(8,128)(2,1)} %param.10, bf16[1024,7168]{1,0:T(8,128)(2,1)S(1)} %bitcast.46, s32[]{:T(128)S(6)} %select_n.221), kind=kOutput, calls=%fused_computation.66 | convolution fusion | flops 1879179264 | bytes 11272196 | tf_op jit(solution)/shard_map/dot_general | solution.py:173
  119.5 5.9 %fusion.98 = bf16[256,512]{1,0:T(8,128)(2,1)} fusion(bf16[7168,2048]{1,0:T(8,128)(2,1)} %param.10, bf16[1024,7168]{1,0:T(8,128)(2,1)S(1)} %bitcast.46, s32[]{:T(128)S(6)} %select_n.250), kind=kOutput, calls=%fused_computation.67 | convolution fusion | flops 1879179264 | bytes 11272196 | tf_op jit(solution)/shard_map/dot_general | solution.py:173
  125.4 6.0 %fusion.108 = bf16[256,512]{1,0:T(8,128)(2,1)} fusion(bf16[7168,2048]{1,0:T(8,128)(2,1)} %param.10, bf16[1024,7168]{1,0:T(8,128)(2,1)S(1)} %bitcast.46, s32[]{:T(128)S(6)} %select_n.249), kind=kOutput, calls=%fused_computation.69 | convolution fusion | flops 1879179264 | bytes 11272196 | tf_op jit(solution)/shard_map/dot_general | solution.py:173
  131.4 5.9 %fusion.118 = bf16[256,512]{1,0:T(8,128)(2,1)} fusion(bf16[7168,2048]{1,0:T(8,128)(2,1)} %param.10, bf16[1024,7168]{1,0:T(8,128)(2,1)S(1)} %bitcast.46, s32[]{:T(128)S(6)} %select_n.250), kind=kOutput, calls=%fused_computation.71 | convolution fusion | flops 1879179264 | bytes 11272196 | tf_op jit(solution)/shard_map/dot_general | solution.py:173
  137.3 5.8 %fusion.123 = bf16[256,512]{1,0:T(8,128)(2,1)} fusion(bf16[7168,2048]{1,0:T(8,128)(2,1)} %param.10, bf16[1024,7168]{1,0:T(8,128)(2,1)S(1)} %bitcast.46, s32[]{:T(128)S(6)} %select_n.251), kind=kOutput, calls=%fused_computation.72 | convolution fusion | flops 1879179264 | bytes 11272196 | tf_op jit(solution)/shard_map/dot_general | solution.py:173
  146.2 7.0 %fusion.113 = bf16[256,512]{1,0:T(8,128)(2,1)} fusion(bf16[7168,2048]{1,0:T(8,128)(2,1)} %param.10, bf16[1024,7168]{1,0:T(8,128)(2,1)} %hidden_ref.1, s32[]{:T(128)S(6)} %select_n.221), kind=kOutput, calls=%fused_computation.70 | convolution fusion | flops 1879179264 | bytes 11272196 | tf_op jit(solution)/shard_map/dot_general | solution.py:173
  175.5 3.8 %collective-permute-start.30 = (bf16[256,512]{1,0:T(8,128)(2,1)}, bf16[256,512]{1,0:T(8,128)(2,1)S(1)}, u32[]{:S(2)}, u32[]{:S(2)}) collective-permute-start(bf16[256,512]{1,0:T(8,128)(2,1)} %fusion.103), channel_id=1, source_target_pairs={{0,4},{12,8},{1,5},{13,9},{2,6},{14,10},{3,7},{15,11},{16,20},{28,... | collective-permute-start | bytes 786440 | tf_op jit(solution)/shard_map/ppermute | solution.py:222
  181.2 3.7 %collective-permute-start.28 = (bf16[256,512]{1,0:T(8,128)(2,1)S(1)}, bf16[256,512]{1,0:T(8,128)(2,1)S(1)}, u32[]{:S(2)}, u32[]{:S(2)}) collective-permute-start(bf16[256,512]{1,0:T(8,128)(2,1)S(1)} %copy-done.11), channel_id=1, source_target_pairs={{0,4},{12,8},{1,5},{13,9},{2,6},{14,10},{3,7},{15,11},{16,20},{28,... | collective-permute-start | bytes 786440 | tf_op jit(solution)/shard_map/ppermute | solution.py:222
  191.9 4.2 %collective-permute-start.36 = (bf16[256,512]{1,0:T(8,128)(2,1)}, bf16[256,512]{1,0:T(8,128)(2,1)S(1)}, u32[]{:S(2)}, u32[]{:S(2)}) collective-permute-start(bf16[256,512]{1,0:T(8,128)(2,1)} %fusion.123), channel_id=1, source_target_pairs={{0,4},{12,8},{1,5},{13,9},{2,6},{14,10},{3,7},{15,11},{16,20},{28,... | collective-permute-start | bytes 786440 | tf_op jit(solution)/shard_map/ppermute | solution.py:222
  201.3 4.6 %collective-permute-start.9 = (bf16[128,2048]{1,0:T(8,128)(2,1)S(1)}, bf16[128,2048]{1,0:T(8,128)(2,1)S(1)}, u32[]{:S(2)}, u32[]{:S(2)}) collective-permute-start(bf16[128,2048]{1,0:T(8,128)(2,1)S(1)} %add_bitcast_fusion), channel_id=1, source_target_pairs={{0,4},{4,8},{8,12},{1,5},{5,9},{9,13},{2,6},{6,10},{10,14},{3,7},{... | collective-permute-start | bytes 1572872 | tf_op jit(solution)/shard_map/ppermute | solution.py:140
  211.4 3.8 %collective-permute-done.10 = bf16[128,2048]{1,0:T(8,128)(2,1)S(1)} collective-permute-done((bf16[128,2048]{1,0:T(8,128)(2,1)S(1)}, bf16[128,2048]{1,0:T(8,128)(2,1)S(1)}, u32[]{:S(2)}, u32[]{:S(2)}) %collective-permute-start.10) | collective-permute-done | bytes 524320 | tf_op jit(solution)/shard_map/ppermute | solution.py:141
  221.6 9.0 %collective-permute-done.11 = bf16[128,2048]{1,0:T(8,128)(2,1)S(1)} collective-permute-done((bf16[128,2048]{1,0:T(8,128)(2,1)S(1)}, bf16[128,2048]{1,0:T(8,128)(2,1)S(1)}, u32[]{:S(2)}, u32[]{:S(2)}) %collective-permute-start.11) | collective-permute-done | bytes 524320 | tf_op jit(solution)/shard_map/ppermute | solution.py:141
  233.7 15.2 %collective-permute-start.21 = (bf16[256,512]{1,0:T(8,128)(2,1)}, bf16[256,512]{1,0:T(8,128)(2,1)S(1)}, u32[]{:S(2)}, u32[]{:S(2)}) collective-permute-start(bf16[256,512]{1,0:T(8,128)(2,1)} %fusion.73), channel_id=1, source_target_pairs={{0,4},{12,8},{1,5},{13,9},{2,6},{14,10},{3,7},{15,11},{16,20},{28,... | collective-permute-start | bytes 786440 | tf_op jit(solution)/shard_map/ppermute | solution.py:222
  249.9 3.8 %collective-permute-start.27 = (bf16[256,512]{1,0:T(8,128)(2,1)S(1)}, bf16[256,512]{1,0:T(8,128)(2,1)S(1)}, u32[]{:S(2)}, u32[]{:S(2)}) collective-permute-start(bf16[256,512]{1,0:T(8,128)(2,1)S(1)} %copy-done.9), channel_id=1, source_target_pairs={{0,4},{12,8},{1,5},{13,9},{2,6},{14,10},{3,7},{15,11},{16,20},{28,... | collective-permute-start | bytes 786440 | tf_op jit(solution)/shard_map/ppermute | solution.py:222
  259.0 5.0 %collective-permute-start.33 = (bf16[256,512]{1,0:T(8,128)(2,1)S(1)}, bf16[256,512]{1,0:T(8,128)(2,1)S(1)}, u32[]{:S(2)}, u32[]{:S(2)}) collective-permute-start(bf16[256,512]{1,0:T(8,128)(2,1)S(1)} %copy-done.10), channel_id=1, source_target_pairs={{0,4},{12,8},{1,5},{13,9},{2,6},{14,10},{3,7},{15,11},{16,20},{28,... | collective-permute-start | bytes 786440 | tf_op jit(solution)/shard_map/ppermute | solution.py:222
  269.6 4.8 %collective-permute-done.26 = bf16[256,512]{1,0:T(8,128)(2,1)S(1)} collective-permute-done((bf16[256,512]{1,0:T(8,128)(2,1)S(1)}, bf16[256,512]{1,0:T(8,128)(2,1)S(1)}, u32[]{:S(2)}, u32[]{:S(2)}) %collective-permute-start.26) | collective-permute-done | bytes 262176 | tf_op jit(solution)/shard_map/ppermute | solution.py:222
  277.2 7.8 %collective-permute-done.32 = bf16[256,512]{1,0:T(8,128)(2,1)S(1)} collective-permute-done((bf16[256,512]{1,0:T(8,128)(2,1)S(1)}, bf16[256,512]{1,0:T(8,128)(2,1)S(1)}, u32[]{:S(2)}, u32[]{:S(2)}) %collective-permute-start.32) | collective-permute-done | bytes 262176 | tf_op jit(solution)/shard_map/ppermute | solution.py:222
  (191 shorter events, 83.7 us)
Async XLA Ops:
  9.2 249.8 %collective-permute-start.15 = (bf16[256,512]{1,0:T(8,128)(2,1)}, bf16[256,512]{1,0:T(8,128)(2,1)}, u32[]{:S(2)}, u32[]{:S(2)}) collective-permute-start(bf16[256,512]{1,0:T(8,128)(2,1)} %fusion.48), channel_id=1, source_target_pairs={{0,4},{12,8},{1,5},{13,9},{2,6},{14,10},{3,7},{15,11},{16,20},{28,... | collective-permute-start | bytes 786440 | tf_op jit(solution)/shard_map/ppermute | solution.py:222
  36.5 106.6 %collective-permute-start = (bf16[4,2,64,128]{3,2,1,0:T(8,128)(2,1)S(1)}, bf16[4,2,64,128]{3,2,1,0:T(8,128)(2,1)}, u32[]{:S(2)}, u32[]{:S(2)}) collective-permute-start(bf16[4,2,64,128]{3,2,1,0:T(8,128)(2,1)S(1)} %dynamic-slice_bitcast_fusion), channel_id=1, source_target_pairs={{0,1},{1,0},{2,3},{3,2},{4,5},{5,4},{6,7},{7,6},{8,9},{9,8},{10,11... | collective-permute-start | bytes 393224 | tf_op jit(solution)/shard_map/ppermute | solution.py:96
  52.1 134.5 %collective-permute-start.7 = (bf16[128,2,2048]{2,0,1:T(8,128)(2,1)S(1)}, bf16[128,2,2048]{2,0,1:T(8,128)(2,1)}, u32[]{:S(2)}, u32[]{:S(2)}) collective-permute-start(bf16[128,2,2048]{2,0,1:T(8,128)(2,1)S(1)} %bitcast.48), channel_id=1, source_target_pairs={{0,1},{1,0},{2,3},{3,2},{4,5},{5,4},{6,7},{7,6},{8,9},{9,8},{10,11... | collective-permute-start | bytes 3145736 | tf_op jit(solution)/shard_map/ppermute | solution.py:96
  144.7 9.1 %collective-permute-start.1 = (bf16[4,1,64,128]{3,2,1,0:T(8,128)(2,1)}, bf16[4,1,64,128]{3,2,1,0:T(8,128)(2,1)}, u32[]{:S(2)}, u32[]{:S(2)}) collective-permute-start(bf16[4,1,64,128]{3,2,1,0:T(8,128)(2,1)} %constant_dynamic-slice_fusion.7), channel_id=1, source_target_pairs={{0,2},{1,3},{2,0},{3,1},{4,6},{5,7},{6,4},{7,5},{8,10},{9,11},{10,... | collective-permute-start | bytes 196616 | tf_op jit(solution)/shard_map/ppermute | solution.py:96
  160.8 10.1 %collective-permute-start.18 = (bf16[256,512]{1,0:T(8,128)(2,1)}, bf16[256,512]{1,0:T(8,128)(2,1)}, u32[]{:S(2)}, u32[]{:S(2)}) collective-permute-start(bf16[256,512]{1,0:T(8,128)(2,1)} %fusion.63), channel_id=1, source_target_pairs={{0,4},{12,8},{1,5},{13,9},{2,6},{14,10},{3,7},{15,11},{16,20},{28,... | collective-permute-start | bytes 786440 | tf_op jit(solution)/shard_map/ppermute | solution.py:222
  163.0 12.5 %collective-permute-start.16 = (bf16[256,512]{1,0:T(8,128)(2,1)}, bf16[256,512]{1,0:T(8,128)(2,1)}, u32[]{:S(2)}, u32[]{:S(2)}) collective-permute-start(bf16[256,512]{1,0:T(8,128)(2,1)} %fusion.58), channel_id=1, source_target_pairs={{0,4},{12,8},{1,5},{13,9},{2,6},{14,10},{3,7},{15,11},{16,20},{28,... | collective-permute-start | bytes 786440 | tf_op jit(solution)/shard_map/ppermute | solution.py:222
  169.5 11.6 %collective-permute-start.24 = (bf16[256,512]{1,0:T(8,128)(2,1)}, bf16[256,512]{1,0:T(8,128)(2,1)S(1)}, u32[]{:S(2)}, u32[]{:S(2)}) collective-permute-start(bf16[256,512]{1,0:T(8,128)(2,1)} %fusion.83), channel_id=1, source_target_pairs={{0,4},{12,8},{1,5},{13,9},{2,6},{14,10},{3,7},{15,11},{16,20},{28,... | collective-permute-start | bytes 786440 | tf_op jit(solution)/shard_map/ppermute | solution.py:222
  170.9 19.5 %collective-permute-start.22 = (bf16[256,512]{1,0:T(8,128)(2,1)}, bf16[256,512]{1,0:T(8,128)(2,1)S(1)}, u32[]{:S(2)}, u32[]{:S(2)}) collective-permute-start(bf16[256,512]{1,0:T(8,128)(2,1)} %fusion.78), channel_id=1, source_target_pairs={{0,4},{12,8},{1,5},{13,9},{2,6},{14,10},{3,7},{15,11},{16,20},{28,... | collective-permute-start | bytes 786440 | tf_op jit(solution)/shard_map/ppermute | solution.py:222
  175.5 16.4 %collective-permute-start.30 = (bf16[256,512]{1,0:T(8,128)(2,1)}, bf16[256,512]{1,0:T(8,128)(2,1)S(1)}, u32[]{:S(2)}, u32[]{:S(2)}) collective-permute-start(bf16[256,512]{1,0:T(8,128)(2,1)} %fusion.103), channel_id=1, source_target_pairs={{0,4},{12,8},{1,5},{13,9},{2,6},{14,10},{3,7},{15,11},{16,20},{28,... | collective-permute-start | bytes 786440 | tf_op jit(solution)/shard_map/ppermute | solution.py:222
  181.2 16.1 %collective-permute-start.28 = (bf16[256,512]{1,0:T(8,128)(2,1)S(1)}, bf16[256,512]{1,0:T(8,128)(2,1)S(1)}, u32[]{:S(2)}, u32[]{:S(2)}) collective-permute-start(bf16[256,512]{1,0:T(8,128)(2,1)S(1)} %copy-done.11), channel_id=1, source_target_pairs={{0,4},{12,8},{1,5},{13,9},{2,6},{14,10},{3,7},{15,11},{16,20},{28,... | collective-permute-start | bytes 786440 | tf_op jit(solution)/shard_map/ppermute | solution.py:222
  186.6 19.3 %collective-permute-start.34 = (bf16[256,512]{1,0:T(8,128)(2,1)}, bf16[256,512]{1,0:T(8,128)(2,1)S(1)}, u32[]{:S(2)}, u32[]{:S(2)}) collective-permute-start(bf16[256,512]{1,0:T(8,128)(2,1)} %fusion.118), channel_id=1, source_target_pairs={{0,4},{12,8},{1,5},{13,9},{2,6},{14,10},{3,7},{15,11},{16,20},{28,... | collective-permute-start | bytes 786440 | tf_op jit(solution)/shard_map/ppermute | solution.py:222
  190.4 9.5 %collective-permute-start.8 = (bf16[128,1,2048]{2,0,1:T(8,128)(2,1)S(1)}, bf16[128,1,2048]{2,0,1:T(8,128)(2,1)S(1)}, u32[]{:S(2)}, u32[]{:S(2)}) collective-permute-start(bf16[128,1,2048]{2,0,1:T(8,128)(2,1)S(1)} %constant_dynamic-slice_fusion), channel_id=1, source_target_pairs={{0,2},{1,3},{2,0},{3,1},{4,6},{5,7},{6,4},{7,5},{8,10},{9,11},{10,... | collective-permute-start | bytes 1572872 | tf_op jit(solution)/shard_map/ppermute | solution.py:96
  191.9 17.1 %collective-permute-start.36 = (bf16[256,512]{1,0:T(8,128)(2,1)}, bf16[256,512]{1,0:T(8,128)(2,1)S(1)}, u32[]{:S(2)}, u32[]{:S(2)}) collective-permute-start(bf16[256,512]{1,0:T(8,128)(2,1)} %fusion.123), channel_id=1, source_target_pairs={{0,4},{12,8},{1,5},{13,9},{2,6},{14,10},{3,7},{15,11},{16,20},{28,... | collective-permute-start | bytes 786440 | tf_op jit(solution)/shard_map/ppermute | solution.py:222
  200.0 15.2 %collective-permute-start.10 = (bf16[128,2048]{1,0:T(8,128)(2,1)S(1)}, bf16[128,2048]{1,0:T(8,128)(2,1)S(1)}, u32[]{:S(2)}, u32[]{:S(2)}) collective-permute-start(bf16[128,2048]{1,0:T(8,128)(2,1)S(1)} %add_bitcast_fusion), channel_id=1, source_target_pairs={{12,8},{8,4},{4,0},{13,9},{9,5},{5,1},{14,10},{10,6},{6,2},{15,11}... | collective-permute-start | bytes 1572872 | tf_op jit(solution)/shard_map/ppermute | solution.py:141
  201.3 16.4 %collective-permute-start.9 = (bf16[128,2048]{1,0:T(8,128)(2,1)S(1)}, bf16[128,2048]{1,0:T(8,128)(2,1)S(1)}, u32[]{:S(2)}, u32[]{:S(2)}) collective-permute-start(bf16[128,2048]{1,0:T(8,128)(2,1)S(1)} %add_bitcast_fusion), channel_id=1, source_target_pairs={{0,4},{4,8},{8,12},{1,5},{5,9},{9,13},{2,6},{6,10},{10,14},{3,7},{... | collective-permute-start | bytes 1572872 | tf_op jit(solution)/shard_map/ppermute | solution.py:140
  205.9 13.1 %collective-permute-start.19 = (bf16[256,512]{1,0:T(8,128)(2,1)}, bf16[256,512]{1,0:T(8,128)(2,1)}, u32[]{:S(2)}, u32[]{:S(2)}) collective-permute-start(bf16[256,512]{1,0:T(8,128)(2,1)} %add_convert_fusion.14), channel_id=1, source_target_pairs={{4,8},{8,4},{5,9},{9,5},{6,10},{10,6},{7,11},{11,7},{20,24},{24,20... | collective-permute-start | bytes 786440 | tf_op jit(solution)/shard_map/ppermute | solution.py:222
  209.0 11.9 %collective-permute-start.25 = (bf16[256,512]{1,0:T(8,128)(2,1)}, bf16[256,512]{1,0:T(8,128)(2,1)}, u32[]{:S(2)}, u32[]{:S(2)}) collective-permute-start(bf16[256,512]{1,0:T(8,128)(2,1)} %add_convert_fusion.10), channel_id=1, source_target_pairs={{4,8},{8,4},{5,9},{9,5},{6,10},{10,6},{7,11},{11,7},{20,24},{24,20... | collective-permute-start | bytes 786440 | tf_op jit(solution)/shard_map/ppermute | solution.py:222
  215.2 15.4 %collective-permute-start.11 = (bf16[128,2048]{1,0:T(8,128)(2,1)S(1)}, bf16[128,2048]{1,0:T(8,128)(2,1)S(1)}, u32[]{:S(2)}, u32[]{:S(2)}) collective-permute-start(bf16[128,2048]{1,0:T(8,128)(2,1)S(1)} %collective-permute-done.10), channel_id=1, source_target_pairs={{8,4},{4,0},{9,5},{5,1},{10,6},{6,2},{11,7},{7,3},{24,20},{20,16},... | collective-permute-start | bytes 1572872 | tf_op jit(solution)/shard_map/ppermute | solution.py:141
  217.7 14.2 %collective-permute-start.13 = (bf16[128,2048]{1,0:T(8,128)(2,1)S(1)}, bf16[128,2048]{1,0:T(8,128)(2,1)S(1)}, u32[]{:S(2)}, u32[]{:S(2)}) collective-permute-start(bf16[128,2048]{1,0:T(8,128)(2,1)S(1)} %collective-permute-done.9), channel_id=1, source_target_pairs={{4,8},{8,12},{5,9},{9,13},{6,10},{10,14},{7,11},{11,15},{20,24},{2... | collective-permute-start | bytes 1572872 | tf_op jit(solution)/shard_map/ppermute | solution.py:140
  219.0 14.7 %collective-permute-start.31 = (bf16[256,512]{1,0:T(8,128)(2,1)}, bf16[256,512]{1,0:T(8,128)(2,1)S(1)}, u32[]{:S(2)}, u32[]{:S(2)}) collective-permute-start(bf16[256,512]{1,0:T(8,128)(2,1)} %add_convert_fusion.6), channel_id=1, source_target_pairs={{4,8},{8,4},{5,9},{9,5},{6,10},{10,6},{7,11},{11,7},{20,24},{24,20... | collective-permute-start | bytes 786440 | tf_op jit(solution)/shard_map/ppermute | solution.py:222
  220.9 29.0 %collective-permute-start.37 = (bf16[256,512]{1,0:T(8,128)(2,1)S(1)}, bf16[256,512]{1,0:T(8,128)(2,1)S(1)}, u32[]{:S(2)}, u32[]{:S(2)}) collective-permute-start(bf16[256,512]{1,0:T(8,128)(2,1)S(1)} %add_convert_fusion.2), channel_id=1, source_target_pairs={{4,8},{8,4},{5,9},{9,5},{6,10},{10,6},{7,11},{11,7},{20,24},{24,20... | collective-permute-start | bytes 786440 | tf_op jit(solution)/shard_map/ppermute | solution.py:222
  230.6 24.3 %collective-permute-start.12 = (bf16[128,2048]{1,0:T(8,128)(2,1)S(1)}, bf16[128,2048]{1,0:T(8,128)(2,1)S(1)}, u32[]{:S(2)}, u32[]{:S(2)}) collective-permute-start(bf16[128,2048]{1,0:T(8,128)(2,1)S(1)} %collective-permute-done.11), channel_id=1, source_target_pairs={{4,0},{5,1},{6,2},{7,3},{20,16},{21,17},{22,18},{23,19}} | collective-permute-start | bytes 1572872 | tf_op jit(solution)/shard_map/ppermute | solution.py:141
  231.9 23.8 %collective-permute-start.14 = (bf16[128,2048]{1,0:T(8,128)(2,1)S(1)}, bf16[128,2048]{1,0:T(8,128)(2,1)S(1)}, u32[]{:S(2)}, u32[]{:S(2)}) collective-permute-start(bf16[128,2048]{1,0:T(8,128)(2,1)S(1)} %collective-permute-done.13), channel_id=1, source_target_pairs={{8,12},{9,13},{10,14},{11,15},{24,28},{25,29},{26,30},{27,31}} | collective-permute-start | bytes 1572872 | tf_op jit(solution)/shard_map/ppermute | solution.py:140
  233.7 34.5 %collective-permute-start.21 = (bf16[256,512]{1,0:T(8,128)(2,1)}, bf16[256,512]{1,0:T(8,128)(2,1)S(1)}, u32[]{:S(2)}, u32[]{:S(2)}) collective-permute-start(bf16[256,512]{1,0:T(8,128)(2,1)} %fusion.73), channel_id=1, source_target_pairs={{0,4},{12,8},{1,5},{13,9},{2,6},{14,10},{3,7},{15,11},{16,20},{28,... | collective-permute-start | bytes 786440 | tf_op jit(solution)/shard_map/ppermute | solution.py:222
  249.9 25.9 %collective-permute-start.27 = (bf16[256,512]{1,0:T(8,128)(2,1)S(1)}, bf16[256,512]{1,0:T(8,128)(2,1)S(1)}, u32[]{:S(2)}, u32[]{:S(2)}) collective-permute-start(bf16[256,512]{1,0:T(8,128)(2,1)S(1)} %copy-done.9), channel_id=1, source_target_pairs={{0,4},{12,8},{1,5},{13,9},{2,6},{14,10},{3,7},{15,11},{16,20},{28,... | collective-permute-start | bytes 786440 | tf_op jit(solution)/shard_map/ppermute | solution.py:222
  254.9 9.1 %collective-permute-start.17 = (bf16[256,512]{1,0:T(8,128)(2,1)}, bf16[256,512]{1,0:T(8,128)(2,1)S(1)}, u32[]{:S(2)}, u32[]{:S(2)}) collective-permute-start(bf16[256,512]{1,0:T(8,128)(2,1)} %add_convert_fusion.15), channel_id=1, source_target_pairs={{4,8},{8,4},{5,9},{9,5},{6,10},{10,6},{7,11},{11,7},{20,24},{24,20... | collective-permute-start | bytes 786440 | tf_op jit(solution)/shard_map/ppermute | solution.py:222
  255.7 10.1 %collective-permute-start.20 = (bf16[256,512]{1,0:T(8,128)(2,1)S(1)}, bf16[256,512]{1,0:T(8,128)(2,1)S(1)}, u32[]{:S(2)}, u32[]{:S(2)}) collective-permute-start(bf16[256,512]{1,0:T(8,128)(2,1)S(1)} %add_convert_fusion.13), channel_id=1, source_target_pairs={{8,12},{4,0},{9,13},{5,1},{10,14},{6,2},{11,15},{7,3},{24,28},{20,... | collective-permute-start | bytes 786440 | tf_op jit(solution)/shard_map/ppermute | solution.py:222
  259.0 26.2 %collective-permute-start.33 = (bf16[256,512]{1,0:T(8,128)(2,1)S(1)}, bf16[256,512]{1,0:T(8,128)(2,1)S(1)}, u32[]{:S(2)}, u32[]{:S(2)}) collective-permute-start(bf16[256,512]{1,0:T(8,128)(2,1)S(1)} %copy-done.10), channel_id=1, source_target_pairs={{0,4},{12,8},{1,5},{13,9},{2,6},{14,10},{3,7},{15,11},{16,20},{28,... | collective-permute-start | bytes 786440 | tf_op jit(solution)/shard_map/ppermute | solution.py:222
  268.2 8.9 %collective-permute-start.29 = (bf16[256,512]{1,0:T(8,128)(2,1)S(1)}, bf16[256,512]{1,0:T(8,128)(2,1)S(1)}, u32[]{:S(2)}, u32[]{:S(2)}) collective-permute-start(bf16[256,512]{1,0:T(8,128)(2,1)S(1)} %copy-done.14), channel_id=1, source_target_pairs={{4,8},{8,4},{5,9},{9,5},{6,10},{10,6},{7,11},{11,7},{20,24},{24,20... | collective-permute-start | bytes 786440 | tf_op jit(solution)/shard_map/ppermute | solution.py:222
  268.9 16.2 %collective-permute-start.35 = (bf16[256,512]{1,0:T(8,128)(2,1)S(1)}, bf16[256,512]{1,0:T(8,128)(2,1)S(1)}, u32[]{:S(2)}, u32[]{:S(2)}) collective-permute-start(bf16[256,512]{1,0:T(8,128)(2,1)S(1)} %copy-done.16), channel_id=1, source_target_pairs={{4,8},{8,4},{5,9},{9,5},{6,10},{10,6},{7,11},{11,7},{20,24},{24,20... | collective-permute-start | bytes 786440 | tf_op jit(solution)/shard_map/ppermute | solution.py:222
  274.4 10.6 %collective-permute-start.32 = (bf16[256,512]{1,0:T(8,128)(2,1)S(1)}, bf16[256,512]{1,0:T(8,128)(2,1)S(1)}, u32[]{:S(2)}, u32[]{:S(2)}) collective-permute-start(bf16[256,512]{1,0:T(8,128)(2,1)S(1)} %add_convert_fusion.5), channel_id=1, source_target_pairs={{8,12},{4,0},{9,13},{5,1},{10,14},{6,2},{11,15},{7,3},{24,28},{20,... | collective-permute-start | bytes 786440 | tf_op jit(solution)/shard_map/ppermute | solution.py:222
  275.9 11.9 %collective-permute-start.38 = (bf16[256,512]{1,0:T(8,128)(2,1)S(1)}, bf16[256,512]{1,0:T(8,128)(2,1)S(1)}, u32[]{:S(2)}, u32[]{:S(2)}) collective-permute-start(bf16[256,512]{1,0:T(8,128)(2,1)S(1)} %add_convert_fusion.1), channel_id=1, source_target_pairs={{8,12},{4,0},{9,13},{5,1},{10,14},{6,2},{11,15},{7,3},{24,28},{20,... | collective-permute-start | bytes 786440 | tf_op jit(solution)/shard_map/ppermute | solution.py:222
  (37 other events, 591.0 us)

commit v2 on v1

v2 whole, which is shorter than its diff:
```python
import jax
import jax.numpy as jnp
from jax import lax
from jax.experimental import pallas as pl
from jax.experimental.pallas import tpu as pltpu
from jax.sharding import PartitionSpec as P

VMEM_LIMIT = 52 * 1024 * 1024
LINE = 4


def line_order(n):
    order = []
    for z in range(n):
        sends = [(t, z >= n // 2, n - 1 - t + z) for t in range(z, n - 1)]
        sends += [(t, z < n // 2, t - (n - 1 - z)) for t in range(n - 1 - z, n - 1)]
        order.append([block for _, _, block in sorted(sends)] + [z])
    return order


def first_divisor(size, choices):
    for choice in choices:
        if size % choice == 0:
            return choice
    return size


def after(token, *done):
    return lax.optimization_barrier((token,) + done)[0]


def params():
    return pltpu.CompilerParams(vmem_limit_bytes=VMEM_LIMIT)


def base_kernel(count, place_ref, *refs):
    hidden, matrix, outs, sums = refs[:count], refs[count], refs[count + 1 : -1], refs[-1]
    step = pl.program_id(0)
    rows = jnp.concatenate([ref[...] for ref in hidden], axis=0) if count > 1 else hidden[0][...]
    product = jnp.dot(rows, matrix[...], preferred_element_type=jnp.float32)

    @pl.when(step == 0)
    def _():
        sums[...] = product

    @pl.when(step > 0)
    def _():
        sums[...] += product

    @pl.when(step == pl.num_programs(0) - 1)
    def _():
        block = outs[0].shape[0]
        for i in range(count):
            outs[i][...] = sums[pl.ds(i * block, block), :].astype(outs[i].dtype)


def base_terms(place, hidden, matrix, slots, half, n, halves):
    tokens, depth = hidden.shape
    block, columns = tokens // n, matrix.shape[1] // halves
    tile = first_divisor(depth, (512, 256, 128))
    order = line_order(n)

    def rows_of(slot):
        def index(k, place_ref):
            picked = jnp.int32(order[0][slot])
            for z in range(1, n):
                picked = jnp.where(place_ref[0] == z, order[z][slot], picked)
            return picked, k

        return pl.BlockSpec((block, tile), index)

    count = len(slots)
    return pl.pallas_call(
        lambda *refs: base_kernel(count, *refs),
        out_shape=[jax.ShapeDtypeStruct((block, columns), jnp.bfloat16)] * count,
        grid_spec=pltpu.PrefetchScalarGridSpec(
            num_scalar_prefetch=1,
            grid=(depth // tile,),
            in_specs=[rows_of(slot) for slot in slots] + [pl.BlockSpec((tile, columns), lambda k, _: (k, half))],
            out_specs=[pl.BlockSpec((block, columns), lambda k, _: (0, 0))] * count,
            scratch_shapes=[pltpu.VMEM((count * block, columns), jnp.float32)],
        ),
        compiler_params=params(),
        cost_estimate=pl.CostEstimate(flops=10**6, bytes_accessed=10**5, transcendentals=0),
        name="base_terms",
    )(place, *([hidden] * count), matrix)


def spans(requests_ref, r):
    requests = requests_ref[...]
    return jnp.sum((requests < r).astype(jnp.int32)), jnp.sum((requests <= r).astype(jnp.int32))


def adapter_input_kernel(
    place_ref, request_adapters_ref, ranks_ref, slots_ref, requests_ref, hidden_ref, factor_ref, out_ref, sums_ref
):
    step = pl.program_id(0)
    held, _, width = factor_ref.shape
    factors = jnp.concatenate([factor_ref[s] for s in range(held)], axis=1)
    product = jnp.dot(hidden_ref[...], factors, preferred_element_type=jnp.float32)

    @pl.when(step == 0)
    def _():
        sums_ref[...] = product

    @pl.when(step > 0)
    def _():
        sums_ref[...] += product

    @pl.when(step == pl.num_programs(0) - 1)
    def _():
        row = lax.broadcasted_iota(jnp.int32, out_ref.shape, 0)
        column = lax.broadcasted_iota(jnp.int32, out_ref.shape, 1)
        total = jnp.zeros(out_ref.shape, jnp.float32)
        for r in range(request_adapters_ref.shape[0]):
            adapter = request_adapters_ref[r]
            local_slot = slots_ref[adapter] - place_ref[1] * held
            owned = (local_slot >= 0) & (local_slot < held)
            start, end = spans(requests_ref, r)
            keep = (row >= start) & (row < jnp.where(owned, end, 0)) & (column < ranks_ref[adapter])
            lane = pl.multiple_of(jnp.clip(local_slot, 0, held - 1) * width, width)
            total = jnp.where(keep, sums_ref[:, pl.ds(lane, width)], total)
        out_ref[...] = total.astype(out_ref.dtype)


def adapter_input(place, hidden, factor, token_requests, request_adapters, ranks, slots):
    tokens, depth = hidden.shape
    held, _, width = factor.shape
    tile = first_divisor(depth, (1024, 896, 512, 256, 128))
    smem = pl.BlockSpec(memory_space=pltpu.SMEM)
    return pl.pallas_call(
        adapter_input_kernel,
        out_shape=jax.ShapeDtypeStruct((tokens, width), jnp.bfloat16),
        grid=(depth // tile,),
        in_specs=[
            smem,
            smem,
            smem,
            smem,
            pl.BlockSpec((tokens // 128, 128), lambda k: (0, 0)),
            pl.BlockSpec((tokens, tile), lambda k: (0, k)),
            pl.BlockSpec((held, tile, width), lambda k: (0, k, 0)),
        ],
        out_specs=pl.BlockSpec((tokens, width), lambda k: (0, 0)),
        scratch_shapes=[pltpu.VMEM((tokens, held * width), jnp.float32)],
        compiler_params=params(),
        cost_estimate=pl.CostEstimate(flops=10**6, bytes_accessed=10**5, transcendentals=0),
        name="adapter_input",
    )(place, request_adapters, ranks, slots, token_requests.reshape(tokens // 128, 128), hidden, factor)


def select_rows_kernel(place_ref, request_adapters_ref, slots_ref, kept_in, sent_in, kept_out, sent_out):
    slot = slots_ref[request_adapters_ref[pl.program_id(0)]] - place_ref[1] * place_ref[2]
    owned = (slot >= 0) & (slot < place_ref[2])
    zero = jnp.zeros(kept_out.shape, kept_out.dtype)
    kept_out[...] = jnp.where(owned, kept_in[...], zero)
    sent_out[...] = jnp.where(owned, sent_in[...], zero)


def select_rows(place, factor, request_adapters, slots, shards):
    held, rank_rows, model_width = factor.shape
    requests, width = request_adapters.shape[0], model_width // shards

    def columns_of(other):
        def index(r, i, place_ref, request_adapters_ref, slots_ref):
            slot = slots_ref[request_adapters_ref[r]] - place_ref[1] * held
            side = place_ref[1] % 2
            return jnp.clip(slot, 0, held - 1), 0, 2 * i + (1 - side if other else side)

        return pl.BlockSpec((1, rank_rows, width), index)

    out = jax.ShapeDtypeStruct((requests, rank_rows, shards // 2 * width), factor.dtype)
    return pl.pallas_call(
        select_rows_kernel,
        out_shape=[out, out],
        grid_spec=pltpu.PrefetchScalarGridSpec(
            num_scalar_prefetch=3,
            grid=(requests, shards // 2),
            in_specs=[columns_of(False), columns_of(True)],
            out_specs=[pl.BlockSpec((1, rank_rows, width), lambda r, i, *_: (r, 0, i))] * 2,
        ),
        compiler_params=params(),
        cost_estimate=pl.CostEstimate(flops=10**6, bytes_accessed=10**5, transcendentals=0),
        name="select_rows",
    )(place, request_adapters, slots, factor, factor)


def adapter_term_kernel(
    place_ref, request_adapters_ref, ranks_ref, requests_ref, lora_ref, rows_ref, out_ref
):
    block, width = lora_ref.shape
    row = lax.broadcasted_iota(jnp.int32, (block, width), 0) + place_ref[0] * block
    lora = lora_ref[...].astype(jnp.float32)
    parts = []
    for r in range(request_adapters_ref.shape[0]):
        start, end = spans(requests_ref, r)
        scale = 0.25 * width / ranks_ref[request_adapters_ref[r]].astype(jnp.float32)
        parts.append(jnp.where((row >= start) & (row < end), lora * scale, 0.0).astype(jnp.bfloat16))
    expanded = jnp.concatenate(parts, axis=1)
    out_ref[...] = jnp.dot(expanded, rows_ref[...], preferred_element_type=jnp.float32)


def adapter_term(place, lora, rows, token_requests, request_adapters, ranks):
    block, width = lora.shape
    depth, columns = rows.shape
    tokens = token_requests.shape[0]
    tile = first_divisor(columns, (512, 256, 128))
    smem = pl.BlockSpec(memory_space=pltpu.SMEM)
    return pl.pallas_call(
        adapter_term_kernel,
        out_shape=jax.ShapeDtypeStruct((block, columns), jnp.float32),
        grid=(columns // tile,),
        in_specs=[
            smem,
            smem,
            smem,
            pl.BlockSpec((tokens // 128, 128), lambda j: (0, 0)),
            pl.BlockSpec((block, width), lambda j: (0, 0)),
            pl.BlockSpec((depth, tile), lambda j: (0, j)),
        ],
        out_specs=pl.BlockSpec((block, tile), lambda j: (0, j)),
        compiler_params=params(),
        cost_estimate=pl.CostEstimate(flops=10**6, bytes_accessed=10**5, transcendentals=0),
        name="adapter_term",
    )(place, request_adapters, ranks, token_requests.reshape(tokens // 128, 128), lora, rows)


def swap(x, axis, bit):
    return lax.ppermute(x, axis, [(i, i ^ bit) for i in range(lax.axis_size(axis))])


def bits_of(size):
    return [1 << i for i in range(size.bit_length() - 1)]


def along_edge(x, edge):
    n = lax.axis_size("tensor")
    return lax.ppermute(x, "tensor", [(edge, edge + 1), (n - 1 - edge, n - 2 - edge)])


def sum_halves(x, dim, axis, bit):
    side = (lax.axis_index(axis) // bit) % 2
    size = x.shape[dim] // 2
    kept = lax.dynamic_slice_in_dim(x, side * size, size, dim)
    sent = lax.dynamic_slice_in_dim(x, (1 - side) * size, size, dim)
    return kept + swap(sent, axis, bit)


def join_halves(x, dim, axis, bit):
    other = swap(x, axis, bit)
    high = (lax.axis_index(axis) // bit) % 2 == 1
    return jnp.where(high, jnp.concatenate([other, x], dim), jnp.concatenate([x, other], dim))


def sum_to_blocks(x, axis):
    n = lax.axis_size(axis)
    me = lax.axis_index(axis)
    total = lax.dynamic_index_in_dim(x, me, 0, keepdims=False).astype(jnp.float32)
    for shift in range(1, n):
        sent = lax.dynamic_index_in_dim(x, (me + shift) % n, 0, keepdims=False)
        total += lax.ppermute(sent, axis, [(i, (i + shift) % n) for i in range(n)]).astype(jnp.float32)
    return total.astype(x.dtype)


def place_rows(own, received, place, n):
    full = [jnp.where(place == k, own, jnp.zeros_like(own)) for k in range(n)]
    for j, items in enumerate(received):
        for i in range(j + 1):
            zero = jnp.zeros_like(items[i])
            full[i] += jnp.where(place == j + 1, items[i], zero)
            full[n - 1 - i] += jnp.where(place == n - 2 - j, items[i], zero)
    return jnp.stack(full, axis=1)


def per_device(
    hidden_activations,
    down_matrix,
    adapter_input_factor,
    adapter_output_factor,
    token_requests,
    request_adapters,
    adapter_ranks,
    adapter_store_slot,
):
    n = lax.axis_size("tensor")
    z = lax.axis_index("tensor")
    shards = lax.axis_size("store")
    tokens = hidden_activations.shape[0]
    block = tokens // n
    held, rank_rows, model_width = adapter_output_factor.shape
    width = down_matrix.shape[1]
    requests = request_adapters.shape[0]
    lora_width = adapter_input_factor.shape[2]
    order = line_order(n)
    token = jnp.stack([z, lax.axis_index("store"), jnp.int32(held)]).astype(jnp.int32)
    on_line = n == LINE

    def base(token, slots, half):
        return base_terms(token, hidden_activations, down_matrix, slots, half, n, 2)

    def hop(token, term, came):
        term, came, _ = lax.optimization_barrier((term, came, token))
        return (term.astype(jnp.float32) + came.astype(jnp.float32)).astype(jnp.bfloat16)

    def input_product(token):
        return adapter_input(
            token,
            hidden_activations,
            adapter_input_factor,
            token_requests,
            request_adapters,
            adapter_ranks,
            adapter_store_slot,
        )

    store_bits = bits_of(shards)
    came, terms = {}, {}

    if on_line:
        terms[0, 0], = base(token, [0], 0)
        token = after(token, terms[0, 0])
        came[0, 0, 0] = along_edge(terms[0, 0], 0)
        terms[0, 1], terms[1, 1] = base(token, [0, 1], 1)
        token = after(token, terms[0, 1])
        came[0, 0, 1] = along_edge(terms[0, 1], 0)

    kept, sent = select_rows(token, adapter_output_factor, request_adapters, adapter_store_slot, shards)
    token = after(token, kept, sent)
    swapped = swap(sent, "store", 1)

    if on_line:
        sum_b10 = hop(token, terms[0, 0], came[0, 0, 0])
        token = after(token, sum_b10)
        came[1, 1, 0] = along_edge(sum_b10, 1)
        came[0, 1, 1] = along_edge(after(terms[1, 1], token), 0)

        terms[1, 0], terms[2, 0], terms[3, 0] = base(token, [1, 2, 3], 0)
        token = after(token, terms[1, 0])
        came[0, 1, 0] = along_edge(terms[1, 0], 0)

        sum_b11 = hop(token, terms[0, 1], came[0, 0, 1])
        token = after(token, sum_b11)
        came[1, 1, 1] = along_edge(sum_b11, 1)

    rows = kept + swapped
    for bit in reversed(store_bits[1:]):
        rows = sum_halves(rows, 2, "store", bit)

    partial = input_product(token)
    token = after(token, partial)
    piece = tokens // (n * shards)
    pieces = partial.reshape(n, tokens // n, lora_width)
    pieces = sum_halves(pieces, 1, "store", store_bits[0])

    if on_line:
        sum_c20 = hop(token, terms[2, 0], came[1, 1, 0])
        token = after(token, sum_c20)
        came[2, 2, 0] = along_edge(sum_c20, 2)
        came[0, 2, 0] = along_edge(after(terms[2, 0], token), 0)

        sum_b21 = hop(token, terms[1, 1], came[0, 1, 1])
        token = after(token, sum_b21)
        came[1, 2, 1] = along_edge(sum_b21, 1)

    token, rows, pieces = lax.optimization_barrier((token, rows, pieces))
    received = []
    bundle = rows[None]
    for edge in range(n - 1):
        received.append(along_edge(bundle, edge))
        bundle = jnp.concatenate([received[-1], rows[None]], axis=0)
    for bit in store_bits[1:]:
        pieces = sum_halves(pieces, 1, "store", bit)

    if on_line:
        terms[2, 1], terms[3, 1] = base(token, [2, 3], 1)
        token, pieces = lax.optimization_barrier((token, pieces, terms[2, 1]))[:2]

        sum_c21 = hop(token, terms[2, 1], came[1, 1, 1])
        token = after(token, sum_c21)
        came[2, 2, 1] = along_edge(sum_c21, 2)
        sum_b20 = hop(token, terms[1, 0], came[0, 1, 0])
        token = after(token, sum_b20)
        came[1, 2, 0] = along_edge(sum_b20, 1)
        came[0, 2, 1] = along_edge(after(terms[2, 1], token), 0)

    lora = sum_to_blocks(pieces, "tensor")
    for bit in reversed(store_bits):
        lora = join_halves(lora, 0, "store", bit)
    rows = place_rows(rows, received, z, n).reshape(requests * n * rank_rows, width)
    adapter = adapter_term(token, lora, rows, token_requests, request_adapters, adapter_ranks)

    if on_line:
        outputs = []
        half = width // 2
        adapter, last, _ = lax.optimization_barrier((adapter, came, token))
        for c in range(2):
            total = adapter[:, c * half : (c + 1) * half] + terms[n - 1, c].astype(jnp.float32)
            for edge in range(n - 1):
                total += last[edge, n - 2, c].astype(jnp.float32)
            outputs.append(total.astype(jnp.bfloat16))
        return jnp.concatenate(outputs, axis=1)

    term = jnp.dot(hidden_activations, down_matrix, preferred_element_type=jnp.float32)
    summed = lax.psum_scatter(term.astype(jnp.bfloat16), "tensor", scatter_dimension=0, tiled=True)
    return (summed.astype(jnp.float32) + adapter).astype(jnp.bfloat16)


def solution(mesh):
    in_specs = (
        P("groups", "tensor"),
        P("tensor", "store"),
        P(("groups", "store"), "tensor", None),
        P(("groups", "store"), "tensor", None),
        P("groups"),
        P("groups"),
        P("groups"),
        P("groups"),
    )
    out_specs = P(("groups", "tensor"), "store")
    return jax.shard_map(
        per_device, mesh=mesh, in_specs=in_specs, out_specs=out_specs, check_vma=False
    )
```

time: 295 us -> 219 us (0.74); the launches traced: 289 us -> 217 us
  matrix products: 104 us -> 0 us
  Pallas kernels: 13.3 us -> 98.3 us
  local copies, waits for them, and re-layouts: 25.9 us -> 3.35 us
  waiting for transfers between devices: 37.3 us -> 25 us
  starting transfers between devices: 80.4 us -> 69.5 us
  other arithmetic: 24.9 us -> 20.1 us
  between operations: 3.57 us -> 0.37 us
    dot_general x20 -> x0, matrix products: 104 us -> none  [the longest x16 103 us: base_terms(): jnp.dot(slot_rows(s), matrix, preferred_element_type=jnp.float32)]
    pallas_call x0 -> x6, Pallas kernels: none -> 84.1 us  [the longest x4 73.3 us: base_terms(): pl.pallas_call(lambda *refs: base_kernel(count, *refs), out_shape=[jax.Sh...]
    ppermute x30 -> x15, waiting for transfers between devices: 30.9 us -> 18.3 us  [along_edge(): lax.ppermute(x, 'tensor', [(edge, edge + 1), (n - 1 - edge, n - 2 - edge)])]
    ppermute x30 -> x15, starting transfers between devices: 72.9 us -> 61.5 us  [along_edge(): lax.ppermute(x, 'tensor', [(edge, edge + 1), (n - 1 - edge, n - 2 - edge)])]
    dynamic_slice x5 -> x3, local copies, waits for them, and re-layouts: 8.35 us -> 0.07 us  [sum_halves(): sent = lax.dynamic_slice_in_dim(x, (1 - side) * size, size, dim)]
    unnamed x64 -> x16, local copies, waits for them, and re-layouts: 9.27 us -> 1.69 us
    gather x4 -> x0, local copies, waits for them, and re-layouts: 6.74 us -> none  [the longest x2 5.46 us: per_device(): adapter_output_factor[slot_of % held]]
    convert_element_type x16 -> x6, other arithmetic: 14.7 us -> 10.3 us  [hop(): (term.astype(jnp.float32) + came.astype(jnp.float32)).astype(jnp.bfloat16)]
  transfers between devices with their start and end apart: 39 -> 24, of which waited for: 11 -> 6; matrix products, arithmetic and copies ran while one was open for 47% -> 8% of each run, Pallas kernels for 5% -> 39%
where the time goes in v2:
time: 219 us; the launch traced here: 217 us
  Pallas kernels  98.3 us (45%)
  starting transfers between devices  69.5 us (32%)
  waiting for transfers between devices  25 us (11%)
  other arithmetic  20.1 us (9%)
  local copies, waits for them, and re-layouts  3.35 us (2%)
    pallas_call x4, Pallas kernels, base_terms(): pl.pallas_call(lambda *refs: base_kernel(count, *refs), out_shape=[jax.Sh...  73.3 us
    ppermute x15, starting transfers between devices, along_edge(): lax.ppermute(x, 'tensor', [(edge, edge + 1), (n - 1 - edge, n - 2 - edge)])  61.5 us
    ppermute x15, waiting for transfers between devices, along_edge(): lax.ppermute(x, 'tensor', [(edge, edge + 1), (n - 1 - edge, n - 2 - edge)])  18.3 us
    pallas_call x1, Pallas kernels, adapter_input(): pl.pallas_call(adapter_input_kernel, out_shape=jax.ShapeDtypeStruct((toke...  14.2 us
    convert_element_type x6, other arithmetic, hop(): (term.astype(jnp.float32) + came.astype(jnp.float32)).astype(jnp.bfloat16)  10.3 us
    pallas_call x1, Pallas kernels, select_rows(): pl.pallas_call(select_rows_kernel, out_shape=[out, out], grid_spec=pltpu....  6.22 us
    pallas_call x1, Pallas kernels, adapter_term(): pl.pallas_call(adapter_term_kernel, out_shape=jax.ShapeDtypeStruct((block...  4.63 us
  transfers between devices with their start and end apart: 24, of which 6 were waited for; matrix products, arithmetic and copies ran while one was open for 8% of the time, Pallas kernels for 39%

profile of v2, /device:TPU:0, one launch (start us, length us, event | category | flops | bytes accessed | tf_op | source)
XLA Modules:
  0.0 216.7 jit_solution(4420546773830392526)
XLA Ops:
  0.1 14.7 %base_terms.4 = bf16[256,1024]{1,0:T(8,128)(2,1)S(1)} custom-call(s32[3]{0:T(128)S(1)} %pad_add_fusion.refs_0_.place_ref, bf16[1024,7168]{1,0:T(8,128)(2,1)} %refs_2_.7, bf16[7168,2048]{1,0:T(8,128)(2,1)} %refs_3_.5), custom_call_target="tpu_custom_call" | custom-call | flops 1000000 | bytes 100000 | tf_op jit(solution)/shard_map/base_terms/pallas_call | solution.py:73
  14.8 5.0 %collective-permute-start = (bf16[256,1024]{1,0:T(8,128)(2,1)S(1)}, bf16[256,1024]{1,0:T(8,128)(2,1)S(1)}, u32[]{:S(2)}, u32[]{:S(2)}) collective-permute-start(bf16[256,1024]{1,0:T(8,128)(2,1)S(1)} %base_terms.4), channel_id=1, source_target_pairs={{0,4},{12,8},{1,5},{13,9},{2,6},{14,10},{3,7},{15,11},{16,20},{28,... | collective-permute-start | bytes 1572872 | tf_op jit(solution)/shard_map/ppermute | solution.py:238
  19.8 18.9 %base_terms.5 = (bf16[256,1024]{1,0:T(8,128)(2,1)}, bf16[256,1024]{1,0:T(8,128)(2,1)S(1)}) custom-call(s32[3]{0:T(128)S(1)} %pad_add_fusion.refs_0_.place_ref, bf16[1024,7168]{1,0:T(8,128)(2,1)} %refs_2_.7, bf16[1024,7168]{1,0:T(8,128)(2,1)} %refs_2_.7, bf16[7168,2048]{1,0:T(8,128)(2,1)} %refs_3_.5), custom_call_target="tpu_custom_call" | custom-call | flops 1000000 | bytes 100000 | tf_op jit(solution)/shard_map/base_terms/pallas_call | solution.py:73
  38.7 2.1 collective-permute-start.1
  40.8 6.2 %select_rows.1 = (bf16[4,32,4096]{2,1,0:T(8,128)(2,1)S(1)}, bf16[4,32,4096]{2,1,0:T(8,128)(2,1)}) custom-call(s32[3]{0:T(128)S(1)} %pad_add_fusion.refs_0_.place_ref, s32[4]{0:T(128)S(1)} %copy-done.1, s32[16]{0:T(128)S(1)} %copy-done.2, bf16[4,32,8192]{2,1,0:T(8,128)(2,1)} %sent_in.1, bf16[4,32,8192]{2,1,0:T(8,128)(2,1)} %sent_in.1), custom_call_target="tpu_custom_call" | custom-call | flops 1000000 | bytes 100000 | tf_op jit(solution)/shard_map/select_rows/pallas_call | solution.py:173
  48.0 21.4 %base_terms.6 = (bf16[256,1024]{1,0:T(8,128)(2,1)S(1)}, bf16[256,1024]{1,0:T(8,128)(2,1)S(1)}, bf16[256,1024]{1,0:T(8,128)(2,1)S(1)}) custom-call(s32[3]{0:T(128)S(1)} %pad_add_fusion.refs_0_.place_ref, bf16[1024,7168]{1,0:T(8,128)(2,1)} %refs_2_.7, bf16[1024,7168]{1,0:T(8,128)(2,1)} %refs_2_.7, bf16[1024,7168]{1,0:T(8,128)(2,1)} %refs_2_.7, ...), custom_call_target="tpu_custom_call" | custom-call | flops 1000000 | bytes 100000 | tf_op jit(solution)/shard_map/base_terms/pallas_call | solution.py:73
  69.5 2.2 %add_convert_fusion.6 = bf16[256,1024]{1,0:T(8,128)(2,1)} fusion(bf16[256,1024]{1,0:T(8,128)(2,1)} %collective-permute-done.1, bf16[256,1024]{1,0:T(8,128)(2,1)} %get-tuple-element.63), kind=kLoop, calls=%fused_computation.10 | loop fusion | flops 1048576 | bytes 1572864 | tf_op jit(solution)/shard_map/convert_element_type | solution.py:303
  71.7 14.2 %adapter_input.1 = bf16[1024,128]{1,0:T(8,128)(2,1)S(1)} custom-call(s32[3]{0:T(128)S(1)} %pad_add_fusion.refs_0_.place_ref, s32[4]{0:T(128)S(1)} %copy-done.1, s32[16]{0:T(128)S(1)} %copy-done.3, s32[16]{0:T(128)S(1)} %copy-done.2, s32[8,128]{1,0:T(8,128)S(1)} %bitcast.73, bf16[1024,7168]{1,0:T(8,128)(2,1)} %refs_2_.7, bf16[4,7168,128]{2,1,0:T(8,128)(2,1)} %factor_ref.1), custom_call_target="tpu_custom_call" | custom-call | flops 1000000 | bytes 100000 | tf_op jit(solution)/shard_map/adapter_input/pallas_call | solution.py:131
  86.5 1.4 collective-permute-start.2
  87.9 2.6 %collective-permute-start.3 = (bf16[256,1024]{1,0:T(8,128)(2,1)S(1)}, bf16[256,1024]{1,0:T(8,128)(2,1)S(1)}, u32[]{:S(2)}, u32[]{:S(2)}) collective-permute-start(bf16[256,1024]{1,0:T(8,128)(2,1)S(1)} %get-tuple-element.73), channel_id=1, source_target_pairs={{0,4},{12,8},{1,5},{13,9},{2,6},{14,10},{3,7},{15,11},{16,20},{28,... | collective-permute-start | bytes 1572872 | tf_op jit(solution)/shard_map/ppermute | solution.py:238
  91.5 1.5 add.164
  93.0 1.5 collective-permute-start.5
  94.6 2.0 add_convert_fusion.5
  96.6 5.0 %collective-permute-done.3 = bf16[256,1024]{1,0:T(8,128)(2,1)S(1)} collective-permute-done((bf16[256,1024]{1,0:T(8,128)(2,1)S(1)}, bf16[256,1024]{1,0:T(8,128)(2,1)S(1)}, u32[]{:S(2)}, u32[]{:S(2)}) %collective-permute-start.3) | collective-permute-done | bytes 524320 | tf_op jit(solution)/shard_map/ppermute | solution.py:238
  102.6 3.8 %collective-permute-done.5 = bf16[4,32,2048]{2,1,0:T(8,128)(2,1)S(1)} collective-permute-done((bf16[4,32,2048]{2,1,0:T(8,128)(2,1)S(1)}, bf16[4,32,2048]{2,1,0:T(8,128)(2,1)S(1)}, u32[]{:S(2)}, u32[]{:S(2)}) %collective-permute-start.5) | collective-permute-done | bytes 524320 | tf_op jit(solution)/shard_map/ppermute | solution.py:229
  106.6 1.6 collective-permute-start.15
  108.1 10.2 %collective-permute-done.15 = bf16[1,4,32,2048]{3,2,1,0:T(8,128)(2,1)S(1)} collective-permute-done((bf16[1,4,32,2048]{3,2,1,0:T(8,128)(2,1)S(1)}, bf16[1,4,32,2048]{3,2,1,0:T(8,128)(2,1)S(1)}, u32[]{:S(2)}, u32[]{:S(2)}) %collective-permute-start.15) | collective-permute-done | bytes 524320 | tf_op jit(solution)/shard_map/ppermute | solution.py:238
  123.4 1.5 collective-permute-start.8
  124.9 1.5 collective-permute-start.7
  126.3 32.4 %collective-permute-start.9 = (bf16[256,1024]{1,0:T(8,128)(2,1)S(1)}, bf16[256,1024]{1,0:T(8,128)(2,1)}, u32[]{:S(2)}, u32[]{:S(2)}) collective-permute-start(bf16[256,1024]{1,0:T(8,128)(2,1)S(1)} %get-tuple-element.83), channel_id=1, source_target_pairs={{0,4},{12,8},{1,5},{13,9},{2,6},{14,10},{3,7},{15,11},{16,20},{28,... | collective-permute-start | bytes 1572872 | tf_op jit(solution)/shard_map/ppermute | solution.py:238
  158.7 18.2 %base_terms.7 = (bf16[256,1024]{1,0:T(8,128)(2,1)S(1)}, bf16[256,1024]{1,0:T(8,128)(2,1)S(1)}) custom-call(s32[3]{0:T(128)S(1)} %pad_add_fusion.refs_0_.place_ref, bf16[1024,7168]{1,0:T(8,128)(2,1)} %refs_2_.7, bf16[1024,7168]{1,0:T(8,128)(2,1)} %refs_2_.7, bf16[7168,2048]{1,0:T(8,128)(2,1)} %refs_3_.5), custom_call_target="tpu_custom_call" | custom-call | flops 1000000 | bytes 100000 | tf_op jit(solution)/shard_map/base_terms/pallas_call | solution.py:73
  177.0 3.8 %collective-permute-start.12 = (bf16[64,128]{1,0:T(8,128)(2,1)S(1)}, bf16[64,128]{1,0:T(8,128)(2,1)S(1)}, u32[]{:S(2)}, u32[]{:S(2)}) collective-permute-start(bf16[64,128]{1,0:T(8,128)(2,1)S(1)} %get-tuple-element.106), channel_id=1, source_target_pairs={{0,12},{4,0},{8,4},{12,8},{1,13},{5,1},{9,5},{13,9},{2,14},{6,2},{... | collective-permute-start | bytes 49160 | tf_op jit(solution)/shard_map/ppermute | solution.py:261
  180.8 1.8 collective-permute-done.10
  186.3 2.1 add_convert_fusion.3
  188.3 4.4 %collective-permute-start.18 = (bf16[256,1024]{1,0:T(8,128)(2,1)S(1)}, bf16[256,1024]{1,0:T(8,128)(2,1)S(1)}, u32[]{:S(2)}, u32[]{:S(2)}) collective-permute-start(bf16[256,1024]{1,0:T(8,128)(2,1)S(1)} %get-tuple-element.88), channel_id=1, source_target_pairs={{0,4},{12,8},{1,5},{13,9},{2,6},{14,10},{3,7},{15,11},{16,20},{28,... | collective-permute-start | bytes 1572872 | tf_op jit(solution)/shard_map/ppermute | solution.py:238
  192.9 2.0 add_convert_fusion.2
  196.9 4.6 %collective-permute-start.19 = (bf16[256,1024]{1,0:T(8,128)(2,1)S(1)}, bf16[256,1024]{1,0:T(8,128)(2,1)S(1)}, u32[]{:S(2)}, u32[]{:S(2)}) collective-permute-start(bf16[256,1024]{1,0:T(8,128)(2,1)S(1)} %get-tuple-element.89), channel_id=1, source_target_pairs={{0,4},{12,8},{1,5},{13,9},{2,6},{14,10},{3,7},{15,11},{16,20},{28,... | collective-permute-start | bytes 1572872 | tf_op jit(solution)/shard_map/ppermute | solution.py:238
  201.6 1.8 fusion.3
  203.7 1.6 copy.9
  205.3 4.6 %adapter_term.1 = f32[256,2048]{1,0:T(8,128)} custom-call(s32[3]{0:T(128)S(1)} %pad_add_fusion.refs_0_.place_ref, s32[4]{0:T(128)S(1)} %copy-done.1, s32[16]{0:T(128)S(1)} %copy-done.3, s32[8,128]{1,0:T(8,128)S(1)} %bitcast.74, bf16[256,128]{1,0:T(8,128)(2,1)S(1)} %maximum_select_fusion.lora_ref, bf16[512,2048]{1,0:T(8,128)(2,1)} %bitcast.75), custom_call_target="tpu_custom_call" | custom-call | flops 1000000 | bytes 100000 | tf_op jit(solution)/shard_map/adapter_term/pallas_call | solution.py:209
  209.9 3.2 %collective-permute-done.19 = bf16[256,1024]{1,0:T(8,128)(2,1)S(1)} collective-permute-done((bf16[256,1024]{1,0:T(8,128)(2,1)S(1)}, bf16[256,1024]{1,0:T(8,128)(2,1)S(1)}, u32[]{:S(2)}, u32[]{:S(2)}) %collective-permute-start.19) | collective-permute-done | bytes 524320 | tf_op jit(solution)/shard_map/ppermute | solution.py:238
  213.1 2.6 %add_convert_fusion.1 = (bf16[256,1024]{1,0:T(8,128)(2,1)S(1)}, bf16[256,1024]{1,0:T(8,128)(2,1)S(1)}) fusion(bf16[256,1024]{1,0:T(8,128)(2,1)S(1)} %collective-permute-done.22, bf16[256,1024]{1,0:T(8,128)(2,1)S(1)} %collective-permute-done.20, bf16[256,1024]{1,0:T(8,128)(2,1)S(1)} %collective-permute-done.18, bf16[256,1024]{1,0:T(8,128)(2,1)S(1)} %get-tuple-element.91, ...), kind=kLoop, calls=%fused_computation.5 | loop fusion | flops 4718592 | bytes 7340032 | tf_op jit(solution)/shard_map/convert_element_type | solution.py:400
  (64 shorter events, 16.0 us)
Async XLA Ops:
  14.8 26.0 %copy-start.1 = (s32[4]{0:T(128)S(1)}, s32[4]{0:T(128)}, u32[]{:S(2)}) copy-start(s32[4]{0:T(128)} %request_adapters_ref.5) | copy-start | bytes 52
  14.8 26.0 %copy-start.2 = (s32[16]{0:T(128)S(1)}, s32[16]{0:T(128)}, u32[]{:S(2)}) copy-start(s32[16]{0:T(128)} %slots_ref.3) | copy-start | bytes 196
  14.8 32.2 %collective-permute-start = (bf16[256,1024]{1,0:T(8,128)(2,1)S(1)}, bf16[256,1024]{1,0:T(8,128)(2,1)S(1)}, u32[]{:S(2)}, u32[]{:S(2)}) collective-permute-start(bf16[256,1024]{1,0:T(8,128)(2,1)S(1)} %base_terms.4), channel_id=1, source_target_pairs={{0,4},{12,8},{1,5},{13,9},{2,6},{14,10},{3,7},{15,11},{16,20},{28,... | collective-permute-start | bytes 1572872 | tf_op jit(solution)/shard_map/ppermute | solution.py:238
  38.7 30.8 %collective-permute-start.1 = (bf16[256,1024]{1,0:T(8,128)(2,1)}, bf16[256,1024]{1,0:T(8,128)(2,1)}, u32[]{:S(2)}, u32[]{:S(2)}) collective-permute-start(bf16[256,1024]{1,0:T(8,128)(2,1)} %get-tuple-element.63), channel_id=1, source_target_pairs={{0,4},{12,8},{1,5},{13,9},{2,6},{14,10},{3,7},{15,11},{16,20},{28,... | collective-permute-start | bytes 1572872 | tf_op jit(solution)/shard_map/ppermute | solution.py:238
  47.0 44.5 %collective-permute-start.4 = (bf16[4,32,4096]{2,1,0:T(8,128)(2,1)}, bf16[4,32,4096]{2,1,0:T(8,128)(2,1)}, u32[]{:S(2)}, u32[]{:S(2)}) collective-permute-start(bf16[4,32,4096]{2,1,0:T(8,128)(2,1)} %get-tuple-element.56), channel_id=1, source_target_pairs={{0,1},{1,0},{2,3},{3,2},{4,5},{5,4},{6,7},{7,6},{8,9},{9,8},{10,11... | collective-permute-start | bytes 3145736 | tf_op jit(solution)/shard_map/ppermute | solution.py:229
  48.0 23.7 %copy-start = (s32[1024]{0:T(1024)S(1)}, s32[1024]{0:T(1024)}, u32[]{:S(2)}) copy-start(s32[1024]{0:T(1024)} %param.12) | copy-start | bytes 12292
  48.0 23.7 %copy-start.3 = (s32[16]{0:T(128)S(1)}, s32[16]{0:T(128)}, u32[]{:S(2)}) copy-start(s32[16]{0:T(128)} %ranks_ref.3) | copy-start | bytes 196
  85.9 4.7 %collective-permute-start.6 = (bf16[4,128,128]{2,1,0:T(8,128)(2,1)S(1)}, bf16[4,128,128]{2,1,0:T(8,128)(2,1)}, u32[]{:S(2)}, u32[]{:S(2)}) collective-permute-start(bf16[4,128,128]{2,1,0:T(8,128)(2,1)S(1)} %constant_dynamic-slice_fusion.1), channel_id=1, source_target_pairs={{0,1},{1,0},{2,3},{3,2},{4,5},{5,4},{6,7},{7,6},{8,9},{9,8},{10,11... | collective-permute-start | bytes 393224 | tf_op jit(solution)/shard_map/ppermute | solution.py:229
  86.5 8.1 %collective-permute-start.2 = (bf16[256,1024]{1,0:T(8,128)(2,1)}, bf16[256,1024]{1,0:T(8,128)(2,1)}, u32[]{:S(2)}, u32[]{:S(2)}) collective-permute-start(bf16[256,1024]{1,0:T(8,128)(2,1)} %add_convert_fusion.7), channel_id=1, source_target_pairs={{4,8},{8,4},{5,9},{9,5},{6,10},{10,6},{7,11},{11,7},{20,24},{24,20... | collective-permute-start | bytes 1572872 | tf_op jit(solution)/shard_map/ppermute | solution.py:238
  87.9 13.7 %collective-permute-start.3 = (bf16[256,1024]{1,0:T(8,128)(2,1)S(1)}, bf16[256,1024]{1,0:T(8,128)(2,1)S(1)}, u32[]{:S(2)}, u32[]{:S(2)}) collective-permute-start(bf16[256,1024]{1,0:T(8,128)(2,1)S(1)} %get-tuple-element.73), channel_id=1, source_target_pairs={{0,4},{12,8},{1,5},{13,9},{2,6},{14,10},{3,7},{15,11},{16,20},{28,... | collective-permute-start | bytes 1572872 | tf_op jit(solution)/shard_map/ppermute | solution.py:238
  93.0 13.4 %collective-permute-start.5 = (bf16[4,32,2048]{2,1,0:T(8,128)(2,1)S(1)}, bf16[4,32,2048]{2,1,0:T(8,128)(2,1)S(1)}, u32[]{:S(2)}, u32[]{:S(2)}) collective-permute-start(bf16[4,32,2048]{2,1,0:T(8,128)(2,1)S(1)} %constant_dynamic-slice_fusion.2), channel_id=1, source_target_pairs={{0,2},{1,3},{2,0},{3,1},{4,6},{5,7},{6,4},{7,5},{8,10},{9,11},{10,... | collective-permute-start | bytes 1572872 | tf_op jit(solution)/shard_map/ppermute | solution.py:229
  106.6 11.7 %collective-permute-start.15 = (bf16[1,4,32,2048]{3,2,1,0:T(8,128)(2,1)S(1)}, bf16[1,4,32,2048]{3,2,1,0:T(8,128)(2,1)S(1)}, u32[]{:S(2)}, u32[]{:S(2)}) collective-permute-start(bf16[1,4,32,2048]{3,2,1,0:T(8,128)(2,1)S(1)} %bitcast.76), channel_id=1, source_target_pairs={{0,4},{12,8},{1,5},{13,9},{2,6},{14,10},{3,7},{15,11},{16,20},{28,... | collective-permute-start | bytes 1572872 | tf_op jit(solution)/shard_map/ppermute | solution.py:238
  118.3 0.8 copy-start.6
  119.1 0.7 collective-permute-start.16
  119.8 1.0 copy-start.4
  122.1 74.8 %collective-permute-start.17 = (bf16[3,4,32,2048]{3,2,1,0:T(8,128)(2,1)}, bf16[3,4,32,2048]{3,2,1,0:T(8,128)(2,1)}, u32[]{:S(2)}, u32[]{:S(2)}) collective-permute-start(bf16[3,4,32,2048]{3,2,1,0:T(8,128)(2,1)} %pad_maximum_fusion.1), channel_id=1, source_target_pairs={{8,12},{4,0},{9,13},{5,1},{10,14},{6,2},{11,15},{7,3},{24,28},{20,... | collective-permute-start | bytes 4718600 | tf_op jit(solution)/shard_map/ppermute | solution.py:238
  123.4 57.4 %collective-permute-start.8 = (bf16[256,1024]{1,0:T(8,128)(2,1)}, bf16[256,1024]{1,0:T(8,128)(2,1)}, u32[]{:S(2)}, u32[]{:S(2)}) collective-permute-start(bf16[256,1024]{1,0:T(8,128)(2,1)} %add_convert_fusion.6), channel_id=1, source_target_pairs={{4,8},{8,4},{5,9},{9,5},{6,10},{10,6},{7,11},{11,7},{20,24},{24,20... | collective-permute-start | bytes 1572872 | tf_op jit(solution)/shard_map/ppermute | solution.py:238
  124.9 52.0 %collective-permute-start.7 = (bf16[4,64,128]{2,1,0:T(8,128)(2,1)S(1)}, bf16[4,64,128]{2,1,0:T(8,128)(2,1)S(1)}, u32[]{:S(2)}, u32[]{:S(2)}) collective-permute-start(bf16[4,64,128]{2,1,0:T(8,128)(2,1)S(1)} %constant_dynamic-slice_fusion), channel_id=1, source_target_pairs={{0,2},{1,3},{2,0},{3,1},{4,6},{5,7},{6,4},{7,5},{8,10},{9,11},{10,... | collective-permute-start | bytes 196616 | tf_op jit(solution)/shard_map/ppermute | solution.py:229
  126.3 62.0 %collective-permute-start.9 = (bf16[256,1024]{1,0:T(8,128)(2,1)S(1)}, bf16[256,1024]{1,0:T(8,128)(2,1)}, u32[]{:S(2)}, u32[]{:S(2)}) collective-permute-start(bf16[256,1024]{1,0:T(8,128)(2,1)S(1)} %get-tuple-element.83), channel_id=1, source_target_pairs={{0,4},{12,8},{1,5},{13,9},{2,6},{14,10},{3,7},{15,11},{16,20},{28,... | collective-permute-start | bytes 1572872 | tf_op jit(solution)/shard_map/ppermute | solution.py:238
  176.9 5.7 %collective-permute-start.10 = (bf16[64,128]{1,0:T(8,128)(2,1)S(1)}, bf16[64,128]{1,0:T(8,128)(2,1)S(1)}, u32[]{:S(2)}, u32[]{:S(2)}) collective-permute-start(bf16[64,128]{1,0:T(8,128)(2,1)S(1)} %get-tuple-element.105), channel_id=1, source_target_pairs={{0,4},{4,8},{8,12},{12,0},{1,5},{5,9},{9,13},{13,1},{2,6},{6,10},{... | collective-permute-start | bytes 49160 | tf_op jit(solution)/shard_map/ppermute | solution.py:261
  177.0 6.3 %collective-permute-start.12 = (bf16[64,128]{1,0:T(8,128)(2,1)S(1)}, bf16[64,128]{1,0:T(8,128)(2,1)S(1)}, u32[]{:S(2)}, u32[]{:S(2)}) collective-permute-start(bf16[64,128]{1,0:T(8,128)(2,1)S(1)} %get-tuple-element.106), channel_id=1, source_target_pairs={{0,12},{4,0},{8,4},{12,8},{1,13},{5,1},{9,5},{13,9},{2,14},{6,2},{... | collective-permute-start | bytes 49160 | tf_op jit(solution)/shard_map/ppermute | solution.py:261
  180.8 4.9 %collective-permute-start.11 = (bf16[64,128]{1,0:T(8,128)(2,1)S(1)}, bf16[64,128]{1,0:T(8,128)(2,1)S(1)}, u32[]{:S(2)}, u32[]{:S(2)}) collective-permute-start(bf16[64,128]{1,0:T(8,128)(2,1)S(1)} %get-tuple-element.107), channel_id=1, source_target_pairs={{0,8},{4,12},{8,0},{12,4},{1,9},{5,13},{9,1},{13,5},{2,10},{6,14},... | collective-permute-start | bytes 49160 | tf_op jit(solution)/shard_map/ppermute | solution.py:261
  180.8 20.7 %copy-start.5 = (bf16[2,4,32,2048]{3,2,1,0:T(8,128)(2,1)S(1)}, bf16[2,4,32,2048]{3,2,1,0:T(8,128)(2,1)}, u32[]{:S(2)}) copy-start(bf16[2,4,32,2048]{3,2,1,0:T(8,128)(2,1)} %copy-done.4) | copy-start | bytes 3145732
  180.8 20.7 %copy-start.7 = (bf16[1,4,32,2048]{3,2,1,0:T(8,128)(2,1)S(1)}, bf16[1,4,32,2048]{3,2,1,0:T(8,128)(2,1)}, u32[]{:S(2)}) copy-start(bf16[1,4,32,2048]{3,2,1,0:T(8,128)(2,1)} %copy-done.6) | copy-start | bytes 1572868
  182.6 13.0 %collective-permute-start.21 = (bf16[256,1024]{1,0:T(8,128)(2,1)}, bf16[256,1024]{1,0:T(8,128)(2,1)S(1)}, u32[]{:S(2)}, u32[]{:S(2)}) collective-permute-start(bf16[256,1024]{1,0:T(8,128)(2,1)} %add_convert_fusion.4), channel_id=1, source_target_pairs={{4,8},{8,4},{5,9},{9,5},{6,10},{10,6},{7,11},{11,7},{20,24},{24,20... | collective-permute-start | bytes 1572872 | tf_op jit(solution)/shard_map/ppermute | solution.py:238
  183.3 26.5 %collective-permute-start.22 = (bf16[256,1024]{1,0:T(8,128)(2,1)}, bf16[256,1024]{1,0:T(8,128)(2,1)S(1)}, u32[]{:S(2)}, u32[]{:S(2)}) collective-permute-start(bf16[256,1024]{1,0:T(8,128)(2,1)} %add_convert_fusion.5), channel_id=1, source_target_pairs={{8,12},{4,0},{9,13},{5,1},{10,14},{6,2},{11,15},{7,3},{24,28},{20,... | collective-permute-start | bytes 1572872 | tf_op jit(solution)/shard_map/ppermute | solution.py:238
  185.7 7.0 %collective-permute-start.13 = (bf16[64,128]{1,0:T(8,128)(2,1)S(1)}, bf16[64,128]{1,0:T(8,128)(2,1)S(1)}, u32[]{:S(2)}, u32[]{:S(2)}) collective-permute-start(bf16[64,128]{1,0:T(8,128)(2,1)S(1)} %fusion.6), channel_id=1, source_target_pairs={{0,2},{1,3},{2,0},{3,1},{4,6},{5,7},{6,4},{7,5},{8,10},{9,11},{10,... | collective-permute-start | bytes 49160 | tf_op jit(solution)/shard_map/ppermute | solution.py:229
  188.3 21.5 %collective-permute-start.18 = (bf16[256,1024]{1,0:T(8,128)(2,1)S(1)}, bf16[256,1024]{1,0:T(8,128)(2,1)S(1)}, u32[]{:S(2)}, u32[]{:S(2)}) collective-permute-start(bf16[256,1024]{1,0:T(8,128)(2,1)S(1)} %get-tuple-element.88), channel_id=1, source_target_pairs={{0,4},{12,8},{1,5},{13,9},{2,6},{14,10},{3,7},{15,11},{16,20},{28,... | collective-permute-start | bytes 1572872 | tf_op jit(solution)/shard_map/ppermute | solution.py:238
  192.8 2.1 collective-permute-start.14
  194.9 18.2 %collective-permute-start.20 = (bf16[256,1024]{1,0:T(8,128)(2,1)}, bf16[256,1024]{1,0:T(8,128)(2,1)S(1)}, u32[]{:S(2)}, u32[]{:S(2)}) collective-permute-start(bf16[256,1024]{1,0:T(8,128)(2,1)} %add_convert_fusion.2), channel_id=1, source_target_pairs={{4,8},{8,4},{5,9},{9,5},{6,10},{10,6},{7,11},{11,7},{20,24},{24,20... | collective-permute-start | bytes 1572872 | tf_op jit(solution)/shard_map/ppermute | solution.py:238
  195.6 17.4 %collective-permute-start.23 = (bf16[256,1024]{1,0:T(8,128)(2,1)}, bf16[256,1024]{1,0:T(8,128)(2,1)S(1)}, u32[]{:S(2)}, u32[]{:S(2)}) collective-permute-start(bf16[256,1024]{1,0:T(8,128)(2,1)} %add_convert_fusion.3), channel_id=1, source_target_pairs={{8,12},{4,0},{9,13},{5,1},{10,14},{6,2},{11,15},{7,3},{24,28},{20,... | collective-permute-start | bytes 1572872 | tf_op jit(solution)/shard_map/ppermute | solution.py:238
  196.9 16.1 %collective-permute-start.19 = (bf16[256,1024]{1,0:T(8,128)(2,1)S(1)}, bf16[256,1024]{1,0:T(8,128)(2,1)S(1)}, u32[]{:S(2)}, u32[]{:S(2)}) collective-permute-start(bf16[256,1024]{1,0:T(8,128)(2,1)S(1)} %get-tuple-element.89), channel_id=1, source_target_pairs={{0,4},{12,8},{1,5},{13,9},{2,6},{14,10},{3,7},{15,11},{16,20},{28,... | collective-permute-start | bytes 1572872 | tf_op jit(solution)/shard_map/ppermute | solution.py:238

commit v3 on v0

v3 whole, which is shorter than its diff:
```python
import jax
import jax.numpy as jnp
from jax import lax
from jax.experimental import pallas as pl
from jax.experimental.pallas import tpu as pltpu
from jax.sharding import PartitionSpec as P

VMEM_LIMIT = 52 * 1024 * 1024
LINE = 4
LANES = 128
AHEAD = 4
PAIRS = 2


def line_order(n):
    order = []
    for z in range(n):
        sends = [(t, z >= n // 2, n - 1 - t + z) for t in range(z, n - 1)]
        sends += [(t, z < n // 2, t - (n - 1 - z)) for t in range(n - 1 - z, n - 1)]
        order.append([block for _, _, block in sorted(sends)] + [z])
    return order


def first_divisor(size, choices):
    for choice in choices:
        if size % choice == 0:
            return choice
    return size


def after(token, *done):
    return lax.optimization_barrier((token, done))[0]


def params():
    return pltpu.CompilerParams(vmem_limit_bytes=VMEM_LIMIT)


def small_cost():
    return pl.CostEstimate(flops=10**6, bytes_accessed=10**5, transcendentals=0)


def block_at(order, slot, place):
    picked = jnp.int32(order[0][slot])
    for z in range(1, len(order)):
        picked = jnp.where(place == z, order[z][slot], picked)
    return picked


def spans(requests_ref, r):
    requests = requests_ref[...]
    return jnp.sum((requests < r).astype(jnp.int32)), jnp.sum((requests <= r).astype(jnp.int32))


def adapter_inputs(sums, first_row, meta, requests_ref, held, width):
    place_ref, request_adapters_ref, ranks_ref, slots_ref = meta
    shape = (sums[0].shape[0], width)
    row = lax.broadcasted_iota(jnp.int32, shape, 0) + first_row
    column = lax.broadcasted_iota(jnp.int32, shape, 1)
    total = jnp.zeros(shape, jnp.float32)
    for r in range(request_adapters_ref.shape[0]):
        adapter = request_adapters_ref[r]
        local_slot = slots_ref[adapter] - place_ref[1] * held
        start, end = spans(requests_ref, r)
        for s in range(held):
            last = jnp.where(local_slot == s, end, 0)
            keep = (row >= start) & (row < last) & (column < ranks_ref[adapter])
            total = jnp.where(keep, sums[s], total)
    return total


def base_kernel(order, slots, half, held, *refs):
    meta, refs = refs[:4], refs[4:]
    count = len(slots)
    requests_ref, hidden, matrix, refs = refs[0], refs[1], refs[2], refs[3:]
    factor, refs = (refs[0], refs[1:]) if held else (None, refs)
    outs, (rows, right, sums, sems) = refs[:count], refs[count:]
    steps, _, tile = rows.shape
    columns = outs[0].shape[1]
    block = rows.shape[1] // count
    first_rows = [pl.multiple_of(block_at(order, slot, meta[0][0]) * block, block) for slot in slots]

    def copies(k):
        depth = pl.ds(pl.multiple_of(k * tile, tile), tile)
        moves = [
            (hidden.at[pl.ds(first_rows[i], block), depth], rows.at[k, pl.ds(i * block, block), :])
            for i in range(count)
        ]
        moves.append((matrix.at[depth, pl.ds(half * columns, columns)], right.at[k, :, pl.ds(0, columns)]))
        for s in range(held):
            width = factor.shape[2]
            moves.append((factor.at[s, depth, :], right.at[k, :, pl.ds(columns + s * width, width)]))
        return [pltpu.make_async_copy(a, b, sems.at[k, i]) for i, (a, b) in enumerate(moves)]

    def start(k):
        for copy in copies(k):
            copy.start()

    for k in range(min(AHEAD, steps)):
        start(k)
    sums[...] = jnp.zeros_like(sums)

    def step(k, _):
        @pl.when(k + AHEAD < steps)
        def _():
            start(k + AHEAD)

        for copy in copies(k):
            copy.wait()
        sums[...] += jnp.dot(rows[k], right[k], preferred_element_type=jnp.float32)
        return 0

    lax.fori_loop(0, steps, step, 0)
    for i in range(count):
        own = pl.ds(i * block, block)
        outs[i][:block, :] = sums[own, :columns].astype(jnp.bfloat16)
        if held:
            width = factor.shape[2]
            products = [sums[own, columns + s * width : columns + (s + 1) * width] for s in range(held)]
            inputs = adapter_inputs(products, first_rows[i], meta, requests_ref, held, width).astype(jnp.bfloat16)
            per_row = columns // width
            for j in range(per_row):
                size = block // per_row
                outs[i][block:, j * width : (j + 1) * width] = inputs[j * size : (j + 1) * size, :]


def base_terms(meta, requests, hidden, matrix, factor, slots, half, n):
    tokens, depth = hidden.shape
    block, columns = tokens // n, matrix.shape[1] // 2
    tile = first_divisor(depth, (512, 256, 128))
    steps = depth // tile
    count = len(slots)
    held, width = (factor.shape[0], factor.shape[2]) if factor is not None else (0, 0)
    out_rows = block + block * width // columns
    smem = pl.BlockSpec(memory_space=pltpu.SMEM)
    vmem = pl.BlockSpec(memory_space=pltpu.VMEM)
    hbm = pl.BlockSpec(memory_space=pltpu.HBM)
    arrays = [hidden, matrix] + ([factor] if held else [])
    return pl.pallas_call(
        lambda *refs: base_kernel(line_order(n), slots, half, held, *refs),
        out_shape=[jax.ShapeDtypeStruct((out_rows, columns), jnp.bfloat16)] * count,
        in_specs=[smem] * 4 + [vmem] + [hbm] * len(arrays),
        out_specs=[vmem] * count,
        scratch_shapes=[
            pltpu.VMEM((steps, count * block, tile), jnp.bfloat16),
            pltpu.VMEM((steps, tile, columns + held * width), jnp.bfloat16),
            pltpu.VMEM((count * block, columns + held * width), jnp.float32),
            pltpu.SemaphoreType.DMA((steps, count + 1 + held)),
        ],
        compiler_params=params(),
        cost_estimate=small_cost(),
        name="base_terms",
    )(*meta, requests, *arrays)


def select_rows_kernel(place_ref, request_adapters_ref, slots_ref, factor, kept, sent):
    held = factor.shape[0]
    shards = 2 * PAIRS
    width = factor.shape[2] // shards
    side = place_ref[1] % 2
    for r in range(request_adapters_ref.shape[0]):
        slot = slots_ref[request_adapters_ref[r]] - place_ref[1] * held
        owned = (slot >= 0) & (slot < held)
        slot = jnp.clip(slot, 0, held - 1)
        for out, core in ((kept, side), (sent, 1 - side)):
            for i in range(PAIRS):
                rows = factor[slot, :, pl.ds(pl.multiple_of((2 * i + core) * width, LANES), width)]
                out[r, :, i * width : (i + 1) * width] = jnp.where(owned, rows, jnp.zeros_like(rows))


def select_rows(meta, factor):
    place, request_adapters, _, slots = meta
    _, rank_rows, model_width = factor.shape
    smem = pl.BlockSpec(memory_space=pltpu.SMEM)
    vmem = pl.BlockSpec(memory_space=pltpu.VMEM)
    out = jax.ShapeDtypeStruct((request_adapters.shape[0], rank_rows, model_width // 2), factor.dtype)
    return pl.pallas_call(
        select_rows_kernel,
        out_shape=[out, out],
        in_specs=[smem, smem, smem, vmem],
        out_specs=[vmem, vmem],
        compiler_params=params(),
        cost_estimate=small_cost(),
        name="select_rows",
    )(place, request_adapters, slots, factor)


def expanded_inputs(meta, requests_ref, lora_ref):
    place_ref, request_adapters_ref, ranks_ref, _ = meta
    block, width = lora_ref.shape
    row = lax.broadcasted_iota(jnp.int32, (block, width), 0) + place_ref[0] * block
    lora = lora_ref[...].astype(jnp.float32)
    parts = []
    for r in range(request_adapters_ref.shape[0]):
        start, end = spans(requests_ref, r)
        scale = 0.25 * width / ranks_ref[request_adapters_ref[r]].astype(jnp.float32)
        parts.append(jnp.where((row >= start) & (row < end), lora * scale, 0.0).astype(jnp.bfloat16))
    return jnp.concatenate(parts, axis=1)


def finish_kernel(items, n, *refs):
    meta, requests_ref, lora_ref, refs = refs[:4], refs[4], refs[5], refs[6:]
    pieces, refs = refs[: len(items)], refs[len(items) :]
    added, out, rows = refs[:-2], refs[-2], refs[-1]
    place = meta[0][0]
    requests, rank_rows, width = pieces[0].shape
    rank = n * rank_rows
    for piece, (edge, item) in zip(pieces, items):
        if edge is None:
            targets = [(place >= 0, place)]
        else:
            targets = [(place == edge + 1, item), (place == n - 2 - edge, n - 1 - item)]
        for here, k in targets:

            @pl.when(here)
            def _(piece=piece, k=k):
                for r in range(requests):
                    first = pl.multiple_of(r * rank + k * rank_rows, rank_rows)
                    rows[pl.ds(first, rank_rows), :] = piece[r]

    expanded = expanded_inputs(meta, requests_ref, lora_ref)
    block = lora_ref.shape[0]
    half = width // 2
    for c in range(2):
        columns = slice(c * half, (c + 1) * half)
        total = jnp.dot(expanded, rows[:, columns], preferred_element_type=jnp.float32)
        for ref, which in zip(added, (0, 0, 0, 0, 1, 1)):
            if which == c:
                total += ref[:block, :].astype(jnp.float32)
        out[:, columns] = total.astype(out.dtype)


def finish(meta, requests, lora, items, pieces, added, n):
    smem = pl.BlockSpec(memory_space=pltpu.SMEM)
    vmem = pl.BlockSpec(memory_space=pltpu.VMEM)
    count, rank_rows, width = pieces[0].shape
    return pl.pallas_call(
        lambda *refs: finish_kernel(items, n, *refs),
        out_shape=jax.ShapeDtypeStruct((lora.shape[0], width), jnp.bfloat16),
        in_specs=[smem] * 4 + [vmem] * (2 + len(pieces) + len(added)),
        out_specs=vmem,
        scratch_shapes=[pltpu.VMEM((count * n * rank_rows, width), jnp.bfloat16)],
        compiler_params=params(),
        cost_estimate=small_cost(),
        name="finish",
    )(*meta, requests, lora, *pieces, *added)


def add_last_kernel(total, up, down, out):
    out[...] = (
        total[...].astype(jnp.float32) + up[...].astype(jnp.float32) + down[...].astype(jnp.float32)
    ).astype(out.dtype)


def add_last(total, up, down):
    block, width = total.shape
    half = width // 2
    tile = first_divisor(block, (64, 32, 16))
    arrival = pl.BlockSpec((tile, half), lambda i: (i, 0))
    second = pl.BlockSpec((tile, half), lambda i: (i, 1))
    return pl.pallas_call(
        add_last_kernel,
        out_shape=jax.ShapeDtypeStruct(total.shape, total.dtype),
        grid=(block // tile,),
        in_specs=[second, arrival, arrival],
        out_specs=second,
        input_output_aliases={0: 0},
        cost_estimate=small_cost(),
        name="add_last",
    )(total, up, down)


def swap(x, axis, bit):
    return lax.ppermute(x, axis, [(i, i ^ bit) for i in range(lax.axis_size(axis))])


def bits_of(size):
    return [1 << i for i in range(size.bit_length() - 1)]


def along_edge(x, edge):
    n = lax.axis_size("tensor")
    return lax.ppermute(x, "tensor", [(edge, edge + 1), (n - 1 - edge, n - 2 - edge)])


def take_half(x, dim, side):
    size = x.shape[dim] // 2
    return lax.dynamic_slice_in_dim(x, side * size, size, dim)


def on_line(hidden, matrix, input_factor, output_factor, requests, meta, n):
    shard = lax.axis_index("store")
    token, *rest = meta

    def base(token, slots, half):
        factor = input_factor if half == 0 else None
        return base_terms((token, *rest), requests, hidden, matrix, factor, slots, half, n)

    def hop(token, term, came):
        term, came, _ = lax.optimization_barrier((term, came, token))
        return (term.astype(jnp.float32) + came.astype(jnp.float32)).astype(jnp.bfloat16)

    s, came = {}, {}
    (s[0, 1],) = base(token, [0], 1)
    token = after(token, s[0, 1])
    came[0, 0, 1] = along_edge(s[0, 1], 0)
    kept, sent = select_rows((token, *rest), output_factor)
    token = after(token, kept, sent)
    swapped = swap(sent, "store", 1)
    (s[0, 0],) = base(token, [0], 0)
    token = after(token, s[0, 0])
    came[0, 0, 0] = along_edge(s[0, 0], 0)

    token = after(token, came[0, 0, 1], swapped)
    b11 = hop(token, s[0, 1], came[0, 0, 1])
    came[1, 1, 1] = along_edge(b11, 1)
    rows = kept + swapped
    token = after(token, b11, rows)
    side = shard // 2 % 2
    swapped = swap(take_half(rows, 2, 1 - side), "store", 2)
    rows = take_half(rows, 2, side)

    (s[1, 0],) = base(token, [1], 0)
    token = after(token, s[1, 0])
    came[0, 1, 0] = along_edge(s[1, 0], 0)
    token = after(token, came[0, 0, 0], swapped, came[1, 1, 1])
    b10 = hop(token, s[0, 0], came[0, 0, 0])
    came[1, 1, 0] = along_edge(b10, 1)
    rows = rows + swapped
    token = after(token, b10, rows)
    items = {(edge, edge): along_edge(rows, edge) for edge in range(3)}

    s[2, 0], s[3, 0] = base(token, [2, 3], 0)
    token = after(token, s[2, 0])
    came[0, 2, 0] = along_edge(s[2, 0], 0)
    token = after(token, came[0, 1, 0], came[1, 1, 0], items)
    b20 = hop(token, s[1, 0], came[0, 1, 0])
    came[1, 2, 0] = along_edge(b20, 1)
    c20 = hop(token, s[2, 0], came[1, 1, 0])
    came[2, 2, 0] = along_edge(c20, 2)
    token = after(token, b20, c20)
    items[1, 0] = along_edge(items[0, 0], 1)
    items[2, 1] = along_edge(items[1, 1], 2)

    s[1, 1], s[2, 1], s[3, 1] = base(token, [1, 2, 3], 1)
    token = after(token, s[1, 1])
    came[0, 1, 1] = along_edge(s[1, 1], 0)
    token = after(token, came[0, 2, 0], came[1, 2, 0], came[2, 2, 0], items)
    c21 = hop(token, s[2, 1], came[1, 1, 1])
    token = after(token, c21)
    came[2, 2, 1] = along_edge(c21, 2)
    items[2, 0] = along_edge(items[1, 0], 2)

    block = hidden.shape[0] // n
    width = input_factor.shape[2]
    arrived = [s[3, 0], came[0, 2, 0], came[1, 2, 0], came[2, 2, 0]]
    lora = sum(x[block:].astype(jnp.float32) for x in arrived).astype(jnp.bfloat16)
    lora = lora.reshape(lora.shape[0], -1, width).swapaxes(0, 1).reshape(block, width)
    lora = lora + swap(lora, "store", 1)
    token = after(token, lora)
    came[0, 2, 1] = along_edge(after(s[2, 1], token), 0)
    lora = lora + swap(lora, "store", 2)
    token = after(token, lora, came[0, 1, 1])
    b21 = hop(token, s[1, 1], came[0, 1, 1])
    token = after(token, b21)
    came[1, 2, 1] = along_edge(b21, 1)

    names = list(items)
    added = arrived + [s[3, 1], came[2, 2, 1]]
    out = finish(
        (token, *rest), requests, lora, [(None, None)] + names, [rows] + [items[name] for name in names], added, n
    )
    return add_last(out, came[0, 2, 1], came[1, 2, 1])


def anywhere(hidden, matrix, input_factor, output_factor, token_requests, meta):
    place, request_adapters, ranks, slots = meta
    held = input_factor.shape[0]
    width = input_factor.shape[2]
    rank, slot = ranks[request_adapters], slots[request_adapters]
    owned = slot // held == place[1]
    chosen = token_requests[:, None] == jnp.arange(request_adapters.shape[0])[None, :]
    lora = jnp.zeros((hidden.shape[0], width), jnp.float32)
    for r in range(request_adapters.shape[0]):
        product = jnp.dot(hidden, input_factor[slot[r] % held], preferred_element_type=jnp.float32)
        keep = (chosen[:, r] & owned[r])[:, None] & (jnp.arange(width) < rank[r])[None, :]
        lora = jnp.where(keep, product, lora)
    lora = lax.psum_scatter(lora.astype(jnp.bfloat16), "tensor", scatter_dimension=1, tiled=True)
    lora = lax.psum(lora, "store").astype(jnp.float32)
    rows = jnp.where(owned[:, None, None], output_factor[slot % held], jnp.zeros((), output_factor.dtype))
    rows = lax.psum_scatter(rows, "store", scatter_dimension=2, tiled=True)
    weights = jnp.where(chosen, 0.25 * width / rank.astype(jnp.float32)[None, :], 0.0)
    expanded = (weights[:, :, None] * lora[:, None, :]).reshape(hidden.shape[0], -1).astype(jnp.bfloat16)
    term = jnp.dot(hidden, matrix, preferred_element_type=jnp.float32)
    term += jnp.dot(expanded, rows.reshape(-1, rows.shape[2]), preferred_element_type=jnp.float32)
    return lax.psum_scatter(term.astype(jnp.bfloat16), "tensor", scatter_dimension=0, tiled=True)


def per_device(
    hidden_activations,
    down_matrix,
    adapter_input_factor,
    adapter_output_factor,
    token_requests,
    request_adapters,
    adapter_ranks,
    adapter_store_slot,
):
    n = lax.axis_size("tensor")
    place = jnp.stack([lax.axis_index("tensor"), lax.axis_index("store")]).astype(jnp.int32)
    meta = (place, request_adapters, adapter_ranks, adapter_store_slot)
    arrays = (hidden_activations, down_matrix, adapter_input_factor, adapter_output_factor)
    if n == LINE and lax.axis_size("store") == 2 * PAIRS:
        return on_line(*arrays, token_requests.reshape(-1, LANES), meta, n)
    return anywhere(*arrays, token_requests, meta)


def solution(mesh):
    in_specs = (
        P("groups", "tensor"),
        P("tensor", "store"),
        P(("groups", "store"), "tensor", None),
        P(("groups", "store"), "tensor", None),
        P("groups"),
        P("groups"),
        P("groups"),
        P("groups"),
    )
    out_specs = P(("groups", "tensor"), "store")
    return jax.shard_map(
        per_device, mesh=mesh, in_specs=in_specs, out_specs=out_specs, check_vma=False
    )
```

time: 222 us -> 163 us (0.73)
  waiting for transfers between devices: 120 us -> 33.1 us
  Pallas kernels: 0 us -> 77.1 us
  matrix products: 57.3 us -> 0 us
  starting transfers between devices: 0.12 us -> 38.9 us
  between operations: 13.2 us -> 0.57 us
  loops' own time: 10.4 us -> 0 us
  local copies, waits for them, and re-layouts: 12.4 us -> 6.8 us
  other arithmetic: 9.1 us -> 5.96 us
    reduce_scatter x2 -> x0, waiting for transfers between devices: 99.8 us -> none  [the longest x1 76.9 us: per_device(): lax.psum_scatter((base_product + adapter_product).astype(jnp.bfloat16), '...]
    pallas_call x0 -> x8, Pallas kernels: none -> 77.1 us  [the longest x5 66.1 us: base_terms(): pl.pallas_call(lambda *refs: base_kernel(line_order(n), slots, half, held...]
    dot_general x4 -> x0, matrix products: 57.3 us -> none  [the longest x1 38.4 us: per_device(): jnp.dot(hidden_activations, down_matrix, preferred_element_type=jnp.float32)]
    ppermute x0 -> x22, starting transfers between devices: none -> 38.9 us  [the longest x18 36.3 us: along_edge(): lax.ppermute(x, 'tensor', [(edge, edge + 1), (n - 1 - edge, n - 2 - edge)])]
    ppermute x0 -> x22, waiting for transfers between devices: none -> 33.1 us  [the longest x18 33.1 us: along_edge(): lax.ppermute(x, 'tensor', [(edge, edge + 1), (n - 1 - edge, n - 2 - edge)])]
    unnamed x5 -> x0, waiting for transfers between devices: 20.4 us -> none
    another operation x5 -> x0, loops' own time: 10.4 us -> none  [the longest x4 7.72 us: process_request(): lax.cond(owning_shard[request_number] == store_shard_index, compute_outpu...]
    dynamic_slice x10 -> x1, local copies, waits for them, and re-layouts: 6.36 us -> 0.84 us  [take_half(): return lax.dynamic_slice_in_dim(x, side * size, size, dim)]
  transfers between devices with their start and end apart: 4 -> 22, of which waited for: 3 -> 5; matrix products, arithmetic and copies ran while one was open for 20% -> 4% of each run, Pallas kernels for 0% -> 38%
where the time goes in v3:
time: 163 us; the launch traced here: 162 us
  Pallas kernels  77.1 us (47%)
  starting transfers between devices  38.9 us (24%)
  waiting for transfers between devices  33.1 us (20%)
  local copies, waits for them, and re-layouts  6.8 us (4%)
  other arithmetic  5.96 us (4%)
    pallas_call x5, Pallas kernels, base_terms(): pl.pallas_call(lambda *refs: base_kernel(line_order(n), slots, half, held...  66.1 us
    ppermute x18, starting transfers between devices, along_edge(): lax.ppermute(x, 'tensor', [(edge, edge + 1), (n - 1 - edge, n - 2 - edge)])  36.3 us
    ppermute x18, waiting for transfers between devices, along_edge(): lax.ppermute(x, 'tensor', [(edge, edge + 1), (n - 1 - edge, n - 2 - edge)])  33.1 us
    unnamed x45, local copies, waits for them, and re-layouts  5.95 us
    pallas_call x1, Pallas kernels, finish(): pl.pallas_call(lambda *refs: finish_kernel(items, n, *refs), out_shape=ja...  4.74 us
    pallas_call x1, Pallas kernels, add_last(): pl.pallas_call(add_last_kernel, out_shape=jax.ShapeDtypeStruct(total.shap...  3.49 us
  transfers between devices with their start and end apart: 22, of which 5 were waited for; matrix products, arithmetic and copies ran while one was open for 4% of the time, Pallas kernels for 38%

profile of v3, /device:TPU:0, one launch (start us, length us, event | category | flops | bytes accessed | tf_op | source)
XLA Modules:
  0.0 162.4 jit_solution(1414387812449780571)
XLA Ops:
  2.7 8.4 %base_terms.5 = bf16[256,1024]{1,0:T(8,128)(2,1)S(1)} custom-call(s32[2]{0:T(128)S(1)} %pad_add_fusion.refs_0_.place_ref, s32[4]{0:T(128)S(1)} %copy-done.4, s32[16]{0:T(128)S(1)} %copy-done.8, s32[16]{0:T(128)S(1)} %copy-done.6, s32[8,128]{1,0:T(8,128)S(1)} %bitcast.10, bf16[1024,7168]{1,0:T(8,128)(2,1)} %refs_5_.9, bf16[7168,2048]{1,0:T(8,128)(2,1)} %refs_6_.9), custom_call_target="tpu_custom_call" | custom-call | flops 1000000 | bytes 100000 | tf_op jit(solution)/shard_map/base_terms/pallas_call | solution.py:139
  11.2 2.8 %select_rows.1 = (bf16[4,32,4096]{2,1,0:T(8,128)(2,1)S(1)}, bf16[4,32,4096]{2,1,0:T(8,128)(2,1)}) custom-call(s32[2]{0:T(128)S(1)} %pad_add_fusion.refs_0_.place_ref, s32[4]{0:T(128)S(1)} %copy-done.4, s32[16]{0:T(128)S(1)} %copy-done.6, bf16[4,32,8192]{2,1,0:T(8,128)(2,1)} %factor.1), custom_call_target="tpu_custom_call" | custom-call | flops 1000000 | bytes 100000 | tf_op jit(solution)/shard_map/select_rows/pallas_call | solution.py:177
  14.4 4.5 %collective-permute-start = (bf16[256,1024]{1,0:T(8,128)(2,1)S(1)}, bf16[256,1024]{1,0:T(8,128)(2,1)S(1)}, u32[]{:S(2)}, u32[]{:S(2)}) collective-permute-start(bf16[256,1024]{1,0:T(8,128)(2,1)S(1)} %base_terms.5), channel_id=1, source_target_pairs={{0,4},{12,8},{1,5},{13,9},{2,6},{14,10},{3,7},{15,11},{16,20},{28,... | collective-permute-start | bytes 1572872 | tf_op jit(solution)/shard_map/ppermute | solution.py:283
  18.9 11.5 %base_terms.6 = bf16[288,1024]{1,0:T(8,128)(2,1)S(1)} custom-call(s32[2]{0:T(128)S(1)} %pad_add_fusion.refs_0_.place_ref, s32[4]{0:T(128)S(1)} %copy-done.4, s32[16]{0:T(128)S(1)} %copy-done.8, s32[16]{0:T(128)S(1)} %copy-done.6, s32[8,128]{1,0:T(8,128)S(1)} %bitcast.11, bf16[1024,7168]{1,0:T(8,128)(2,1)} %refs_5_.9, bf16[7168,2048]{1,0:T(8,128)(2,1)} %refs_6_.9, ...), custom_call_target="tpu_custom_call" | custom-call | flops 1000000 | bytes 100000 | tf_op jit(solution)/shard_map/base_terms/pallas_call | solution.py:139
  30.5 2.1 %collective-permute-start.2 = (bf16[288,1024]{1,0:T(8,128)(2,1)S(1)}, bf16[288,1024]{1,0:T(8,128)(2,1)}, u32[]{:S(2)}, u32[]{:S(2)}) collective-permute-start(bf16[288,1024]{1,0:T(8,128)(2,1)S(1)} %base_terms.6), channel_id=1, source_target_pairs={{0,4},{12,8},{1,5},{13,9},{2,6},{14,10},{3,7},{15,11},{16,20},{28,... | collective-permute-start | bytes 1769480 | tf_op jit(solution)/shard_map/ppermute | solution.py:283
  33.4 1.5 add.51
  35.0 0.8 constant_dynamic-slice_fusion
  35.8 1.5 collective-permute-start.3
  37.3 1.0 add_convert_fusion.5
  39.1 11.5 %base_terms.7 = bf16[288,1024]{1,0:T(8,128)(2,1)S(1)} custom-call(s32[2]{0:T(128)S(1)} %pad_add_fusion.refs_0_.place_ref, s32[4]{0:T(128)S(1)} %copy-done.5, s32[16]{0:T(128)S(1)} %copy-done.9, s32[16]{0:T(128)S(1)} %copy-done.7, s32[8,128]{1,0:T(8,128)S(1)} %bitcast.12, bf16[1024,7168]{1,0:T(8,128)(2,1)} %refs_5_.9, bf16[7168,2048]{1,0:T(8,128)(2,1)} %refs_6_.9, ...), custom_call_target="tpu_custom_call" | custom-call | flops 1000000 | bytes 100000 | tf_op jit(solution)/shard_map/base_terms/pallas_call | solution.py:139
  50.6 5.3 %collective-permute-start.5 = (bf16[288,1024]{1,0:T(8,128)(2,1)S(1)}, bf16[288,1024]{1,0:T(8,128)(2,1)S(1)}, u32[]{:S(2)}, u32[]{:S(2)}) collective-permute-start(bf16[288,1024]{1,0:T(8,128)(2,1)S(1)} %base_terms.7), channel_id=1, source_target_pairs={{0,4},{12,8},{1,5},{13,9},{2,6},{14,10},{3,7},{15,11},{16,20},{28,... | collective-permute-start | bytes 1769480 | tf_op jit(solution)/shard_map/ppermute | solution.py:283
  56.0 1.3 add_convert_fusion.2
  58.0 1.2 dynamic-slice_add_fusion.refs_6_
  59.2 1.3 collective-permute-start.9
  61.2 6.3 %collective-permute-start.7 = (bf16[4,32,2048]{2,1,0:T(8,128)(2,1)S(1)}, bf16[4,32,2048]{2,1,0:T(8,128)(2,1)S(1)}, u32[]{:S(2)}, u32[]{:S(2)}) collective-permute-start(bf16[4,32,2048]{2,1,0:T(8,128)(2,1)S(1)} %dynamic-slice_add_fusion.refs_6_), channel_id=1, source_target_pairs={{0,4},{12,8},{1,5},{13,9},{2,6},{14,10},{3,7},{15,11},{16,20},{28,... | collective-permute-start | bytes 1572872 | tf_op jit(solution)/shard_map/ppermute | solution.py:283
  67.5 18.0 %base_terms.8 = (bf16[288,1024]{1,0:T(8,128)(2,1)S(1)}, bf16[288,1024]{1,0:T(8,128)(2,1)S(1)}) custom-call(s32[2]{0:T(128)S(1)} %pad_add_fusion.refs_0_.place_ref, s32[4]{0:T(128)S(1)} %copy-done.5, s32[16]{0:T(128)S(1)} %copy-done.9, s32[16]{0:T(128)S(1)} %copy-done.7, s32[8,128]{1,0:T(8,128)S(1)} %bitcast.13, bf16[1024,7168]{1,0:T(8,128)(2,1)} %refs_5_.9, ...), custom_call_target="tpu_custom_call" | custom-call | flops 1000000 | bytes 100000 | tf_op jit(solution)/shard_map/base_terms/pallas_call | solution.py:139
  85.4 1.3 collective-permute-start.10
  88.0 1.3 collective-permute-start.12
  90.0 1.3 collective-permute-start.14
  91.3 6.5 %collective-permute-done.10.refs_14_ = bf16[288,1024]{1,0:T(8,128)(2,1)S(1)} collective-permute-done((bf16[288,1024]{1,0:T(8,128)(2,1)S(1)}, bf16[288,1024]{1,0:T(8,128)(2,1)S(1)}, u32[]{:S(2)}, u32[]{:S(2)}) %collective-permute-start.10) | collective-permute-done | bytes 589856 | tf_op jit(solution)/shard_map/ppermute | solution.py:283
  97.8 8.4 %collective-permute-done.12.refs_16_ = bf16[288,1024]{1,0:T(8,128)(2,1)S(1)} collective-permute-done((bf16[288,1024]{1,0:T(8,128)(2,1)S(1)}, bf16[288,1024]{1,0:T(8,128)(2,1)S(1)}, u32[]{:S(2)}, u32[]{:S(2)}) %collective-permute-start.12) | collective-permute-done | bytes 589856 | tf_op jit(solution)/shard_map/ppermute | solution.py:283
  106.3 16.6 %base_terms.9 = (bf16[256,1024]{1,0:T(8,128)(2,1)S(1)}, bf16[256,1024]{1,0:T(8,128)(2,1)S(1)}, bf16[256,1024]{1,0:T(8,128)(2,1)S(1)}) custom-call(s32[2]{0:T(128)S(1)} %pad_add_fusion.refs_0_.place_ref, s32[4]{0:T(128)S(1)} %copy-done.5, s32[16]{0:T(128)S(1)} %copy-done.9, s32[16]{0:T(128)S(1)} %copy-done.7, s32[8,128]{1,0:T(8,128)S(1)} %bitcast.14, ...), custom_call_target="tpu_custom_call" | custom-call | flops 1000000 | bytes 100000 | tf_op jit(solution)/shard_map/base_terms/pallas_call | solution.py:139
  123.0 1.5 collective-permute-start.17
  124.5 1.3 collective-permute-start.18
  126.6 1.3 collective-permute-start.19
  127.9 4.6 %collective-permute-start.20 = (bf16[256,1024]{1,0:T(8,128)(2,1)S(1)}, bf16[256,1024]{1,0:T(8,128)(2,1)S(1)}, u32[]{:S(2)}, u32[]{:S(2)}) collective-permute-start(bf16[256,1024]{1,0:T(8,128)(2,1)S(1)} %get-tuple-element.78), channel_id=1, source_target_pairs={{0,4},{12,8},{1,5},{13,9},{2,6},{14,10},{3,7},{15,11},{16,20},{28,... | collective-permute-start | bytes 1572872 | tf_op jit(solution)/shard_map/ppermute | solution.py:283
  132.6 4.0 %collective-permute-done.17 = bf16[256,1024]{1,0:T(8,128)(2,1)S(1)} collective-permute-done((bf16[256,1024]{1,0:T(8,128)(2,1)S(1)}, bf16[256,1024]{1,0:T(8,128)(2,1)S(1)}, u32[]{:S(2)}, u32[]{:S(2)}) %collective-permute-start.17) | collective-permute-done | bytes 524320 | tf_op jit(solution)/shard_map/ppermute | solution.py:283
  137.6 3.6 %collective-permute-done.18.refs_12_ = bf16[4,32,2048]{2,1,0:T(8,128)(2,1)S(1)} collective-permute-done((bf16[4,32,2048]{2,1,0:T(8,128)(2,1)S(1)}, bf16[4,32,2048]{2,1,0:T(8,128)(2,1)S(1)}, u32[]{:S(2)}, u32[]{:S(2)}) %collective-permute-start.18) | collective-permute-done | bytes 524320 | tf_op jit(solution)/shard_map/ppermute | solution.py:283
  141.1 10.7 %collective-permute-done.19.refs_18_ = bf16[256,1024]{1,0:T(8,128)(2,1)S(1)} collective-permute-done((bf16[256,1024]{1,0:T(8,128)(2,1)S(1)}, bf16[256,1024]{1,0:T(8,128)(2,1)S(1)}, u32[]{:S(2)}, u32[]{:S(2)}) %collective-permute-start.19) | collective-permute-done | bytes 524320 | tf_op jit(solution)/shard_map/ppermute | solution.py:283
  152.6 4.7 %finish.1.total = bf16[256,2048]{1,0:T(8,128)(2,1)} custom-call(s32[2]{0:T(128)S(1)} %pad_add_fusion.refs_0_.place_ref, s32[4]{0:T(128)S(1)} %copy-done.5, s32[16]{0:T(128)S(1)} %copy-done.9, s32[16]{0:T(128)S(1)} %copy-done.7, s32[8,128]{1,0:T(8,128)S(1)} %bitcast.15, bf16[256,128]{1,0:T(8,128)(2,1)S(1)} %add.64.refs_5_, ...), custom_call_target="tpu_custom_call" | custom-call | flops 1000000 | bytes 100000 | tf_op jit(solution)/shard_map/finish/pallas_call | solution.py:237
  158.1 0.8 copy-done.21
  159.0 3.5 %add_last.1 = bf16[256,2048]{1,0:T(8,128)(2,1)} custom-call(bf16[256,2048]{1,0:T(8,128)(2,1)} %finish.1.total, bf16[256,1024]{1,0:T(8,128)(2,1)} %copy-done.20, bf16[256,1024]{1,0:T(8,128)(2,1)} %copy-done.21), custom_call_target="tpu_custom_call", output_to_operand_aliasing={{}: (0, {})} | custom-call | flops 1000000 | bytes 100000 | tf_op jit(solution)/shard_map/add_last/pallas_call | solution.py:261
  (79 shorter events, 11.4 us)
Async XLA Ops:
  14.0 19.5 %collective-permute-start.1 = (bf16[4,32,4096]{2,1,0:T(8,128)(2,1)}, bf16[4,32,4096]{2,1,0:T(8,128)(2,1)}, u32[]{:S(2)}, u32[]{:S(2)}) collective-permute-start(bf16[4,32,4096]{2,1,0:T(8,128)(2,1)} %get-tuple-element.44), channel_id=1, source_target_pairs={{0,1},{1,0},{2,3},{3,2},{4,5},{5,4},{6,7},{7,6},{8,9},{9,8},{10,11... | collective-permute-start | bytes 3145736 | tf_op jit(solution)/shard_map/ppermute | solution.py:274
  14.4 18.2 %collective-permute-start = (bf16[256,1024]{1,0:T(8,128)(2,1)S(1)}, bf16[256,1024]{1,0:T(8,128)(2,1)S(1)}, u32[]{:S(2)}, u32[]{:S(2)}) collective-permute-start(bf16[256,1024]{1,0:T(8,128)(2,1)S(1)} %base_terms.5), channel_id=1, source_target_pairs={{0,4},{12,8},{1,5},{13,9},{2,6},{14,10},{3,7},{15,11},{16,20},{28,... | collective-permute-start | bytes 1572872 | tf_op jit(solution)/shard_map/ppermute | solution.py:283
  30.5 25.5 %collective-permute-start.2 = (bf16[288,1024]{1,0:T(8,128)(2,1)S(1)}, bf16[288,1024]{1,0:T(8,128)(2,1)}, u32[]{:S(2)}, u32[]{:S(2)}) collective-permute-start(bf16[288,1024]{1,0:T(8,128)(2,1)S(1)} %base_terms.6), channel_id=1, source_target_pairs={{0,4},{12,8},{1,5},{13,9},{2,6},{14,10},{3,7},{15,11},{16,20},{28,... | collective-permute-start | bytes 1769480 | tf_op jit(solution)/shard_map/ppermute | solution.py:283
  34.9 4.1 %copy-start.3 = (s32[1024]{0:T(1024)S(1)}, s32[1024]{0:T(1024)}, u32[]{:S(2)}) copy-start(s32[1024]{0:T(1024)} %param.12) | copy-start | bytes 12292
  34.9 4.1 %copy-start.5 = (s32[4]{0:T(128)S(1)}, s32[4]{0:T(128)}, u32[]{:S(2)}) copy-start(s32[4]{0:T(128)} %refs_1_.11) | copy-start | bytes 52
  35.8 20.2 %collective-permute-start.3 = (bf16[4,32,2048]{2,1,0:T(8,128)(2,1)}, bf16[4,32,2048]{2,1,0:T(8,128)(2,1)}, u32[]{:S(2)}, u32[]{:S(2)}) collective-permute-start(bf16[4,32,2048]{2,1,0:T(8,128)(2,1)} %constant_dynamic-slice_fusion), channel_id=1, source_target_pairs={{0,2},{1,3},{2,0},{3,1},{4,6},{5,7},{6,4},{7,5},{8,10},{9,11},{10,... | collective-permute-start | bytes 1572872 | tf_op jit(solution)/shard_map/ppermute | solution.py:274
  38.3 17.6 %collective-permute-start.4 = (bf16[256,1024]{1,0:T(8,128)(2,1)}, bf16[256,1024]{1,0:T(8,128)(2,1)S(1)}, u32[]{:S(2)}, u32[]{:S(2)}) collective-permute-start(bf16[256,1024]{1,0:T(8,128)(2,1)} %add_convert_fusion.5), channel_id=1, source_target_pairs={{4,8},{8,4},{5,9},{9,5},{6,10},{10,6},{7,11},{11,7},{20,24},{24,20... | collective-permute-start | bytes 1572872 | tf_op jit(solution)/shard_map/ppermute | solution.py:283
  50.6 34.8 %collective-permute-start.5 = (bf16[288,1024]{1,0:T(8,128)(2,1)S(1)}, bf16[288,1024]{1,0:T(8,128)(2,1)S(1)}, u32[]{:S(2)}, u32[]{:S(2)}) collective-permute-start(bf16[288,1024]{1,0:T(8,128)(2,1)S(1)} %base_terms.7), channel_id=1, source_target_pairs={{0,4},{12,8},{1,5},{13,9},{2,6},{14,10},{3,7},{15,11},{16,20},{28,... | collective-permute-start | bytes 1769480 | tf_op jit(solution)/shard_map/ppermute | solution.py:283
  57.3 29.5 %collective-permute-start.6 = (bf16[288,1024]{1,0:T(8,128)(2,1)S(1)}, bf16[288,1024]{1,0:T(8,128)(2,1)S(1)}, u32[]{:S(2)}, u32[]{:S(2)}) collective-permute-start(bf16[288,1024]{1,0:T(8,128)(2,1)S(1)} %add_convert_fusion.2), channel_id=1, source_target_pairs={{4,8},{8,4},{5,9},{9,5},{6,10},{10,6},{7,11},{11,7},{20,24},{24,20... | collective-permute-start | bytes 1769480 | tf_op jit(solution)/shard_map/ppermute | solution.py:283
  59.2 27.6 %collective-permute-start.9 = (bf16[4,32,2048]{2,1,0:T(8,128)(2,1)S(1)}, bf16[4,32,2048]{2,1,0:T(8,128)(2,1)S(1)}, u32[]{:S(2)}, u32[]{:S(2)}) collective-permute-start(bf16[4,32,2048]{2,1,0:T(8,128)(2,1)S(1)} %dynamic-slice_add_fusion.refs_6_), channel_id=1, source_target_pairs={{8,12},{4,0},{9,13},{5,1},{10,14},{6,2},{11,15},{7,3},{24,28},{20,... | collective-permute-start | bytes 1572872 | tf_op jit(solution)/shard_map/ppermute | solution.py:283
  60.5 26.3 %collective-permute-start.8 = (bf16[4,32,2048]{2,1,0:T(8,128)(2,1)S(1)}, bf16[4,32,2048]{2,1,0:T(8,128)(2,1)S(1)}, u32[]{:S(2)}, u32[]{:S(2)}) collective-permute-start(bf16[4,32,2048]{2,1,0:T(8,128)(2,1)S(1)} %dynamic-slice_add_fusion.refs_6_), channel_id=1, source_target_pairs={{4,8},{8,4},{5,9},{9,5},{6,10},{10,6},{7,11},{11,7},{20,24},{24,20... | collective-permute-start | bytes 1572872 | tf_op jit(solution)/shard_map/ppermute | solution.py:283
  61.2 25.6 %collective-permute-start.7 = (bf16[4,32,2048]{2,1,0:T(8,128)(2,1)S(1)}, bf16[4,32,2048]{2,1,0:T(8,128)(2,1)S(1)}, u32[]{:S(2)}, u32[]{:S(2)}) collective-permute-start(bf16[4,32,2048]{2,1,0:T(8,128)(2,1)S(1)} %dynamic-slice_add_fusion.refs_6_), channel_id=1, source_target_pairs={{0,4},{12,8},{1,5},{13,9},{2,6},{14,10},{3,7},{15,11},{16,20},{28,... | collective-permute-start | bytes 1572872 | tf_op jit(solution)/shard_map/ppermute | solution.py:283
  85.4 20.8 %copy-start = (bf16[288,1024]{1,0:T(8,128)(2,1)}, bf16[288,1024]{1,0:T(8,128)(2,1)S(1)}, u32[]{:S(2)}) copy-start(bf16[288,1024]{1,0:T(8,128)(2,1)S(1)} %get-tuple-element.71.refs_13_) | copy-start | bytes 1769476
  85.4 12.4 %collective-permute-start.10 = (bf16[288,1024]{1,0:T(8,128)(2,1)S(1)}, bf16[288,1024]{1,0:T(8,128)(2,1)S(1)}, u32[]{:S(2)}, u32[]{:S(2)}) collective-permute-start(bf16[288,1024]{1,0:T(8,128)(2,1)S(1)} %get-tuple-element.61), channel_id=1, source_target_pairs={{0,4},{12,8},{1,5},{13,9},{2,6},{14,10},{3,7},{15,11},{16,20},{28,... | collective-permute-start | bytes 1769480 | tf_op jit(solution)/shard_map/ppermute | solution.py:283
  87.1 10.7 %collective-permute-start.11 = (bf16[288,1024]{1,0:T(8,128)(2,1)S(1)}, bf16[288,1024]{1,0:T(8,128)(2,1)S(1)}, u32[]{:S(2)}, u32[]{:S(2)}) collective-permute-start(bf16[288,1024]{1,0:T(8,128)(2,1)S(1)} %add_convert_fusion.1), channel_id=1, source_target_pairs={{4,8},{8,4},{5,9},{9,5},{6,10},{10,6},{7,11},{11,7},{20,24},{24,20... | collective-permute-start | bytes 1769480 | tf_op jit(solution)/shard_map/ppermute | solution.py:283
  88.0 18.2 %collective-permute-start.12 = (bf16[288,1024]{1,0:T(8,128)(2,1)S(1)}, bf16[288,1024]{1,0:T(8,128)(2,1)S(1)}, u32[]{:S(2)}, u32[]{:S(2)}) collective-permute-start(bf16[288,1024]{1,0:T(8,128)(2,1)S(1)} %add_convert_fusion), channel_id=1, source_target_pairs={{8,12},{4,0},{9,13},{5,1},{10,14},{6,2},{11,15},{7,3},{24,28},{20,... | collective-permute-start | bytes 1769480 | tf_op jit(solution)/shard_map/ppermute | solution.py:283
  89.3 35.2 %collective-permute-start.13 = (bf16[4,32,2048]{2,1,0:T(8,128)(2,1)S(1)}, bf16[4,32,2048]{2,1,0:T(8,128)(2,1)S(1)}, u32[]{:S(2)}, u32[]{:S(2)}) collective-permute-start(bf16[4,32,2048]{2,1,0:T(8,128)(2,1)S(1)} %collective-permute-done.7.refs_7_), channel_id=1, source_target_pairs={{4,8},{8,4},{5,9},{9,5},{6,10},{10,6},{7,11},{11,7},{20,24},{24,20... | collective-permute-start | bytes 1572872 | tf_op jit(solution)/shard_map/ppermute | solution.py:283
  90.0 35.8 %collective-permute-start.14 = (bf16[4,32,2048]{2,1,0:T(8,128)(2,1)S(1)}, bf16[4,32,2048]{2,1,0:T(8,128)(2,1)S(1)}, u32[]{:S(2)}, u32[]{:S(2)}) collective-permute-start(bf16[4,32,2048]{2,1,0:T(8,128)(2,1)S(1)} %collective-permute-done.8.refs_8_), channel_id=1, source_target_pairs={{8,12},{4,0},{9,13},{5,1},{10,14},{6,2},{11,15},{7,3},{24,28},{20,... | collective-permute-start | bytes 1572872 | tf_op jit(solution)/shard_map/ppermute | solution.py:283
  97.8 25.1 %copy-start.10 = (bf16[288,1024]{1,0:T(8,128)(2,1)}, bf16[288,1024]{1,0:T(8,128)(2,1)S(1)}, u32[]{:S(2)}) copy-start(bf16[288,1024]{1,0:T(8,128)(2,1)S(1)} %collective-permute-done.10.refs_14_) | copy-start | bytes 1769476
  97.8 25.1 %copy-start.11 = (bf16[288,1024]{1,0:T(8,128)(2,1)}, bf16[288,1024]{1,0:T(8,128)(2,1)S(1)}, u32[]{:S(2)}) copy-start(bf16[288,1024]{1,0:T(8,128)(2,1)S(1)} %collective-permute-done.11.refs_15_) | copy-start | bytes 1769476
  106.2 16.8 %copy-start.12 = (bf16[288,1024]{1,0:T(8,128)(2,1)}, bf16[288,1024]{1,0:T(8,128)(2,1)S(1)}, u32[]{:S(2)}) copy-start(bf16[288,1024]{1,0:T(8,128)(2,1)S(1)} %collective-permute-done.12.refs_16_) | copy-start | bytes 1769476
  106.3 19.6 %collective-permute-start.15 = (bf16[256,128]{1,0:T(8,128)(2,1)S(1)}, bf16[256,128]{1,0:T(8,128)(2,1)S(1)}, u32[]{:S(2)}, u32[]{:S(2)}) collective-permute-start(bf16[256,128]{1,0:T(8,128)(2,1)S(1)} %bitcast.16), channel_id=1, source_target_pairs={{0,1},{1,0},{2,3},{3,2},{4,5},{5,4},{6,7},{7,6},{8,9},{9,8},{10,11... | collective-permute-start | bytes 196616 | tf_op jit(solution)/shard_map/ppermute | solution.py:274
  123.0 13.9 %copy-start.1 = (bf16[256,1024]{1,0:T(8,128)(2,1)}, bf16[256,1024]{1,0:T(8,128)(2,1)S(1)}, u32[]{:S(2)}) copy-start(bf16[256,1024]{1,0:T(8,128)(2,1)S(1)} %get-tuple-element.77.refs_17_) | copy-start | bytes 1572868
  123.0 13.7 %collective-permute-start.17 = (bf16[256,1024]{1,0:T(8,128)(2,1)S(1)}, bf16[256,1024]{1,0:T(8,128)(2,1)S(1)}, u32[]{:S(2)}, u32[]{:S(2)}) collective-permute-start(bf16[256,1024]{1,0:T(8,128)(2,1)S(1)} %get-tuple-element.74), channel_id=1, source_target_pairs={{0,4},{12,8},{1,5},{13,9},{2,6},{14,10},{3,7},{15,11},{16,20},{28,... | collective-permute-start | bytes 1572872 | tf_op jit(solution)/shard_map/ppermute | solution.py:283
  124.5 12.4 %copy-start.14 = (bf16[4,32,2048]{2,1,0:T(8,128)(2,1)}, bf16[4,32,2048]{2,1,0:T(8,128)(2,1)S(1)}, u32[]{:S(2)}) copy-start(bf16[4,32,2048]{2,1,0:T(8,128)(2,1)S(1)} %collective-permute-done.13.refs_10_) | copy-start | bytes 1572868
  124.5 16.6 %collective-permute-start.18 = (bf16[4,32,2048]{2,1,0:T(8,128)(2,1)S(1)}, bf16[4,32,2048]{2,1,0:T(8,128)(2,1)S(1)}, u32[]{:S(2)}, u32[]{:S(2)}) collective-permute-start(bf16[4,32,2048]{2,1,0:T(8,128)(2,1)S(1)} %collective-permute-done.13.refs_10_), channel_id=1, source_target_pairs={{8,12},{4,0},{9,13},{5,1},{10,14},{6,2},{11,15},{7,3},{24,28},{20,... | collective-permute-start | bytes 1572872 | tf_op jit(solution)/shard_map/ppermute | solution.py:283
  125.8 11.1 %copy-start.15 = (bf16[4,32,2048]{2,1,0:T(8,128)(2,1)}, bf16[4,32,2048]{2,1,0:T(8,128)(2,1)S(1)}, u32[]{:S(2)}) copy-start(bf16[4,32,2048]{2,1,0:T(8,128)(2,1)S(1)} %collective-permute-done.14.refs_11_) | copy-start | bytes 1572868
  125.8 6.8 %collective-permute-start.16 = (bf16[256,128]{1,0:T(8,128)(2,1)S(1)}, bf16[256,128]{1,0:T(8,128)(2,1)S(1)}, u32[]{:S(2)}, u32[]{:S(2)}) collective-permute-start(bf16[256,128]{1,0:T(8,128)(2,1)S(1)} %bitcast_add_fusion), channel_id=1, source_target_pairs={{0,2},{1,3},{2,0},{3,1},{4,6},{5,7},{6,4},{7,5},{8,10},{9,11},{10,... | collective-permute-start | bytes 196616 | tf_op jit(solution)/shard_map/ppermute | solution.py:274
  126.6 25.1 %collective-permute-start.19 = (bf16[256,1024]{1,0:T(8,128)(2,1)S(1)}, bf16[256,1024]{1,0:T(8,128)(2,1)S(1)}, u32[]{:S(2)}, u32[]{:S(2)}) collective-permute-start(bf16[256,1024]{1,0:T(8,128)(2,1)S(1)} %add_convert_fusion.4), channel_id=1, source_target_pairs={{8,12},{4,0},{9,13},{5,1},{10,14},{6,2},{11,15},{7,3},{24,28},{20,... | collective-permute-start | bytes 1572872 | tf_op jit(solution)/shard_map/ppermute | solution.py:283
  127.9 29.4 %collective-permute-start.20 = (bf16[256,1024]{1,0:T(8,128)(2,1)S(1)}, bf16[256,1024]{1,0:T(8,128)(2,1)S(1)}, u32[]{:S(2)}, u32[]{:S(2)}) collective-permute-start(bf16[256,1024]{1,0:T(8,128)(2,1)S(1)} %get-tuple-element.78), channel_id=1, source_target_pairs={{0,4},{12,8},{1,5},{13,9},{2,6},{14,10},{3,7},{15,11},{16,20},{28,... | collective-permute-start | bytes 1572872 | tf_op jit(solution)/shard_map/ppermute | solution.py:283
  136.9 20.5 %collective-permute-start.21 = (bf16[256,1024]{1,0:T(8,128)(2,1)S(1)}, bf16[256,1024]{1,0:T(8,128)(2,1)S(1)}, u32[]{:S(2)}, u32[]{:S(2)}) collective-permute-start(bf16[256,1024]{1,0:T(8,128)(2,1)S(1)} %add_convert_fusion.3), channel_id=1, source_target_pairs={{4,8},{8,4},{5,9},{9,5},{6,10},{10,6},{7,11},{11,7},{20,24},{24,20... | collective-permute-start | bytes 1572872 | tf_op jit(solution)/shard_map/ppermute | solution.py:283
  141.1 10.7 %copy-start.18 = (bf16[4,32,2048]{2,1,0:T(8,128)(2,1)}, bf16[4,32,2048]{2,1,0:T(8,128)(2,1)S(1)}, u32[]{:S(2)}) copy-start(bf16[4,32,2048]{2,1,0:T(8,128)(2,1)S(1)} %collective-permute-done.18.refs_12_) | copy-start | bytes 1572868
  (12 other events, 17.7 us)
